TPU v7x, 512 devices: a whole 4x4x16 slice. The times are simulated.
512 devices in a mesh: seq: 16 (over z), chan: 32 (over x, y, core).
Axes of the slice: x: 4, y: 4, z: 16, core: 2. Of those that a mesh axis runs over, the one named last changes fastest.
Arguments:
- features: bfloat16 [3, 128, 131072], P(None, 'chan', 'seq'), may hold values from -6 to 6
- short_taps: float32 [3, 128, 3], P(None, 'chan'), may hold values from -3 to 3
- long_filter: float32 [128, 131072], P('chan', 'seq'), may hold values from -2 to 2
- skip_gain: float32 [128], P('chan'), may hold values from 0.5 to 1.5
- out_weight: bfloat16 [128, 4096], P(None, 'chan'), may hold values from -0.5 to 0.5
Outputs:
- projected: bfloat16 [131072, 4096], P('seq', 'chan')
All inputs are finite; a program needn't handle non-finite values.
Results may differ from a plain program's by a relative error of at most 0.0049.
Values may be sent and summed in bfloat16 or wider, within the bound.
No kernel may reach another device: no remote copies, remote signals or barrier semaphores. Data moves between devices by JAX's collectives and lax.ppermute only.
A program may use at most 64 MiB of HBM per device.

v0:
```python
import math

import jax
import jax.numpy as jnp
from jax import lax
from jax.sharding import PartitionSpec as P

exact_mode = lax.Precision.HIGHEST


def partner_2(block, axis, distance):
    count = lax.axis_size(axis)
    route = []
    for low in range(count):
        high = low | 1 << distance
        if high != low and high < count:
            route += [(low, high), (high, low)]
    return lax.ppermute(block, axis, route)


def passed_along(value, axis, steps):
    count = lax.axis_size(axis)
    initial, last = (max(0, -steps), min(count, count - steps))
    return lax.ppermute(value, axis, [(source, source + steps) for source in range(initial, last)])


def rotation(numerator, denominator, direction):
    angles = jnp.asarray(numerator).astype(jnp.float32) * (direction * 2.0 * math.pi / denominator)
    return (jnp.cos(angles), jnp.sin(angles))


def rotate(signal, cosine, sine_part):
    real_part = signal[0] * cosine - signal[1] * sine_part
    imag_part = signal[0] * sine_part + signal[1] * cosine
    return jnp.stack([real_part, imag_part])


def complex_product(left_side, right_side):
    real_part = left_side[0] * right_side[0] - left_side[1] * right_side[1]
    imag_part = left_side[0] * right_side[1] + left_side[1] * right_side[0]
    return jnp.stack([real_part, imag_part])


def dft_table(extent, direction):
    index_row = jnp.arange(extent, dtype=jnp.int32)
    return rotation(index_row[:, None] * index_row[None, :] % extent, extent, direction)


def left_apply(matrix, signal):
    cosine, sine_part = matrix

    def contract_left(left_side, right_side):
        return jnp.einsum("km,gmn->gkn", left_side, right_side, precision=exact_mode)

    real_part = contract_left(cosine, signal[0]) - contract_left(sine_part, signal[1])
    imag_part = contract_left(cosine, signal[1]) + contract_left(sine_part, signal[0])
    return jnp.stack([real_part, imag_part])


def right_apply(signal, matrix):
    cosine, sine_part = matrix

    def contract_right(left_side, right_side):
        return jnp.einsum("gkm,mn->gkn", left_side, right_side, precision=exact_mode)

    real_part = contract_right(signal[0], cosine) - contract_right(signal[1], sine_part)
    imag_part = contract_right(signal[1], cosine) + contract_right(signal[0], sine_part)
    return jnp.stack([real_part, imag_part])


def local_forward(signal, outer_len, inner_len):
    row_count = signal.shape[1]
    shaped = signal.reshape(2, row_count, outer_len, inner_len)
    shaped = left_apply(dft_table(outer_len, -1.0), shaped)
    freq_rows = jnp.arange(outer_len, dtype=jnp.int32)[:, None]
    time_cols = jnp.arange(inner_len, dtype=jnp.int32)[None, :]
    cosine, sine_part = rotation(freq_rows * time_cols, outer_len * inner_len, -1.0)
    shaped = rotate(shaped, cosine, sine_part)
    return right_apply(shaped, dft_table(inner_len, -1.0))


def local_inverse(spectrum, outer_len, inner_len):
    row_count = spectrum.shape[1]
    shaped = right_apply(spectrum, dft_table(inner_len, 1.0))
    freq_rows = jnp.arange(outer_len, dtype=jnp.int32)[:, None]
    time_cols = jnp.arange(inner_len, dtype=jnp.int32)[None, :]
    cosine, sine_part = rotation(freq_rows * time_cols, outer_len * inner_len, 1.0)
    shaped = rotate(shaped, cosine, sine_part)
    shaped = left_apply(dft_table(outer_len, 1.0), shaped)
    return shaped.reshape(2, row_count, outer_len * inner_len)


def reversed_index(device, bit_count):
    reversed_sum = jnp.zeros((), jnp.int32)
    for bit_place in range(bit_count):
        reversed_sum = reversed_sum + (device >> bit_place & 1) * (1 << bit_count - 1 - bit_place)
    return reversed_sum


def pairs_forward(signal, device_count):
    bit_count = device_count.bit_length() - 1
    device = lax.axis_index("seq")
    for step_index in range(bit_count):
        bit_place = bit_count - 1 - step_index
        half_size = 1 << bit_place
        partner = partner_2(signal, "seq", bit_place)
        upper_bit = device >> bit_place & 1
        lower_part = device & half_size - 1
        sign_factor = (1 - 2 * upper_bit).astype(jnp.float32)
        combined = partner + sign_factor * signal
        cosine, sine_part = rotation(upper_bit * lower_part, 2 * half_size, -1.0)
        signal = rotate(combined, cosine, sine_part)
    return signal


def pairs_inverse(signal, device_count):
    bit_count = device_count.bit_length() - 1
    device = lax.axis_index("seq")
    for bit_place in range(bit_count):
        half_size = 1 << bit_place
        partner = partner_2(signal, "seq", bit_place)
        upper_bit = device >> bit_place & 1
        lower_part = device & half_size - 1
        is_upper = upper_bit == 1
        even_part = jnp.where(is_upper, partner, signal)
        odd_part = jnp.where(is_upper, signal, partner)
        cosine, sine_part = rotation(lower_part, 2 * half_size, 1.0)
        turned = rotate(odd_part, cosine, sine_part)
        sign_factor = (1 - 2 * upper_bit).astype(jnp.float32)
        signal = even_part + sign_factor * turned
    return signal


def shards(features, short_taps, long_filter, skip_gain, out_weight):
    chan_local, tok_local = long_filter.shape
    device_count = lax.axis_size("seq")
    device = lax.axis_index("seq")
    seq_total = tok_local * device_count
    rim_rows = passed_along(features[:, :, tok_local - 2 :], "seq", 1)
    extended = jnp.concatenate([rim_rows, features], axis=2)
    short_mixed = short_taps[:, :, 0:1] * extended[:, :, 2 : 2 + tok_local]
    short_mixed = short_mixed + short_taps[:, :, 1:2] * extended[:, :, 1 : 1 + tok_local]
    short_mixed = short_mixed + short_taps[:, :, 2:3] * extended[:, :, 0:tok_local]
    queries = short_mixed[0]
    product = short_mixed[1] * short_mixed[2]
    local_pos = jnp.arange(tok_local, dtype=jnp.int32)
    positions = device * tok_local + local_pos
    cosine, sine_part = rotation(positions, 2 * seq_total, -1.0)
    zero_rows = jnp.zeros((2 * chan_local, tok_local), jnp.float32)
    plain_rows = jnp.stack([jnp.concatenate([product, long_filter], axis=0), zero_rows])
    twisted = rotate(plain_rows, cosine, sine_part)
    signal = jnp.concatenate([plain_rows, twisted], axis=1)
    signal = pairs_forward(signal, device_count)
    freq_index = reversed_index(device, device_count.bit_length() - 1)
    cosine, sine_part = rotation(local_pos * freq_index, seq_total, -1.0)
    signal = rotate(signal, cosine, sine_part)
    inner_len = min(128, tok_local)
    outer_len = tok_local // inner_len
    spectrum = local_forward(signal, outer_len, inner_len)
    grouped = spectrum.reshape(2, 2, 2, chan_local, outer_len, inner_len)
    data_part = grouped[:, :, 0]
    filter_part = grouped[:, :, 1]
    filtered = complex_product(data_part, filter_part).reshape(
        2, 2 * chan_local, outer_len, inner_len
    )
    time_rows = local_inverse(filtered, outer_len, inner_len)
    cosine, sine_part = rotation(local_pos * freq_index, seq_total, 1.0)
    time_rows = rotate(time_rows, cosine, sine_part)
    time_rows = pairs_inverse(time_rows, device_count)
    halves = time_rows.reshape(2, 2, chan_local, tok_local)
    cosine, sine_part = rotation(positions, 2 * seq_total, 1.0)
    convolved = (halves[0, 0] + halves[0, 1] * cosine - halves[1, 1] * sine_part) / (
        2.0 * seq_total
    )
    gated_rows = (queries * (convolved + skip_gain[:, None] * product)).astype(jnp.bfloat16)
    projected = lax.dot_general(
        lax.all_gather(gated_rows, "chan", axis=0, tiled=True),
        out_weight,
        (((0,), (0,)), ((), ())),
        preferred_element_type=jnp.float32,
    )
    return projected.astype(jnp.bfloat16)


def solution(mesh):
    placed = (
        P(None, "chan", "seq"),
        P(None, "chan", None),
        P("chan", "seq"),
        P("chan"),
        P(None, "chan"),
    )
    return jax.shard_map(
        shards, mesh=mesh, in_specs=placed, out_specs=P("seq", "chan"), check_vma=False
    )
```

profile of v0, /device:TPU:1, one launch (start us, length us, event | category | flops | bytes accessed | tf_op | source)
XLA Modules:
  0.0 516.6 jit_solution(7965174698755615178)
XLA Ops:
  6.5 0.8 slice.150
  7.3 4.4 collective-permute-start
  12.0 0.9 slice_reduce_fusion.2
  13.0 1.5 multiply_add_fusion.9
  14.6 1.0 maximum_bitcast_fusion
  15.8 16.2 %collective-permute-start.1 = (f32[2,16,8192]{2,1,0:T(8,128)S(1)}, f32[2,16,8192]{2,1,0:T(8,128)S(1)}, u32[]{:S(2)}, u32[]{:S(2)}) collective-permute-start(f32[2,16,8192]{2,1,0:T(8,128)S(1)} %select_maximum_fusion), channel_id=1, source_target_pairs={{0,256},{256,0},{32,288},{288,32},{64,320},{320,64},{96,352},{352,... | collective-permute-start | bytes 3145736 | tf_op jit(solution)/shard_map/ppermute | solution.py:18
  32.1 44.7 %collective-permute-done.1 = f32[2,16,8192]{2,1,0:T(8,128)S(1)} collective-permute-done((f32[2,16,8192]{2,1,0:T(8,128)S(1)}, f32[2,16,8192]{2,1,0:T(8,128)S(1)}, u32[]{:S(2)}, u32[]{:S(2)}) %collective-permute-start.1) | collective-permute-done | bytes 1048608 | tf_op jit(solution)/shard_map/ppermute | solution.py:18
  77.0 1.0 pad_maximum_fusion
  78.1 49.6 %collective-permute-start.2 = (f32[2,16,8192]{2,1,0:T(8,128)}, f32[2,16,8192]{2,1,0:T(8,128)S(1)}, u32[]{:S(2)}, u32[]{:S(2)}) collective-permute-start(f32[2,16,8192]{2,1,0:T(8,128)} %pad_maximum_fusion), channel_id=1, source_target_pairs={{0,128},{128,0},{32,160},{160,32},{64,192},{192,64},{96,224},{224,... | collective-permute-start | bytes 3145736 | tf_op jit(solution)/shard_map/ppermute | solution.py:18
  127.8 84.5 %collective-permute-done.2 = f32[2,16,8192]{2,1,0:T(8,128)S(1)} collective-permute-done((f32[2,16,8192]{2,1,0:T(8,128)}, f32[2,16,8192]{2,1,0:T(8,128)S(1)}, u32[]{:S(2)}, u32[]{:S(2)}) %collective-permute-start.2) | collective-permute-done | bytes 1048608 | tf_op jit(solution)/shard_map/ppermute | solution.py:18
  212.5 1.0 pad_maximum_fusion.1
  213.5 1.9 collective-permute-start.3
  215.6 47.5 %collective-permute-done.3 = f32[2,16,8192]{2,1,0:T(8,128)S(1)} collective-permute-done((f32[2,16,8192]{2,1,0:T(8,128)}, f32[2,16,8192]{2,1,0:T(8,128)S(1)}, u32[]{:S(2)}, u32[]{:S(2)}) %collective-permute-start.3) | collective-permute-done | bytes 1048608 | tf_op jit(solution)/shard_map/ppermute | solution.py:18
  263.3 1.0 pad_maximum_fusion.2
  264.4 2.1 collective-permute-start.4
  266.5 0.1 fusion.74
  267.1 23.7 %collective-permute-done.4 = f32[2,16,8192]{2,1,0:T(8,128)S(1)} collective-permute-done((f32[2,16,8192]{2,1,0:T(8,128)}, f32[2,16,8192]{2,1,0:T(8,128)S(1)}, u32[]{:S(2)}, u32[]{:S(2)}) %collective-permute-start.4) | collective-permute-done | bytes 1048608 | tf_op jit(solution)/shard_map/ppermute | solution.py:18
  291.1 0.2 multiply_subtract_fusion.1
  291.4 0.7 fusion.48
  292.1 0.7 fusion.46
  292.8 0.7 fusion.1
  293.6 0.7 fusion
  294.3 0.8 fusion.11
  295.2 0.8 fusion.10
  296.0 0.8 convolution_add_fusion
  296.8 0.8 convolution_subtract_fusion
  297.7 0.6 fusion.24
  298.4 0.6 fusion.26
  299.0 0.6 convolution_add_fusion.3
  299.6 0.6 convolution_subtract_fusion.3
  300.2 0.6 fusion.37
  300.8 0.5 fusion.36
  301.3 0.5 fusion.2
  302.0 0.5 fusion.3
  302.7 2.5 collective-permute-start.5
  305.1 11.5 %collective-permute-done.5 = f32[2,8,8192]{2,1,0:T(8,128)S(1)} collective-permute-done((f32[2,8,8192]{2,1,0:T(8,128)S(1)}, f32[2,8,8192]{2,1,0:T(8,128)S(1)}, u32[]{:S(2)}, u32[]{:S(2)}) %collective-permute-start.5) | collective-permute-done | bytes 524320 | tf_op jit(solution)/shard_map/ppermute | solution.py:18
  316.9 3.3 collective-permute-start.6
  320.3 24.0 %collective-permute-done.6 = f32[2,8,8192]{2,1,0:T(8,128)S(1)} collective-permute-done((f32[2,8,8192]{2,1,0:T(8,128)S(1)}, f32[2,8,8192]{2,1,0:T(8,128)S(1)}, u32[]{:S(2)}, u32[]{:S(2)}) %collective-permute-start.6) | collective-permute-done | bytes 524320 | tf_op jit(solution)/shard_map/ppermute | solution.py:18
  344.6 1.9 collective-permute-start.7
  346.7 61.3 %collective-permute-done.7 = f32[2,8,8192]{2,1,0:T(8,128)S(1)} collective-permute-done((f32[2,8,8192]{2,1,0:T(8,128)S(1)}, f32[2,8,8192]{2,1,0:T(8,128)S(1)}, u32[]{:S(2)}, u32[]{:S(2)}) %collective-permute-start.7) | collective-permute-done | bytes 524320 | tf_op jit(solution)/shard_map/ppermute | solution.py:18
  408.2 6.5 %collective-permute-start.8 = (f32[2,8,8192]{2,1,0:T(8,128)S(1)}, f32[2,8,8192]{2,1,0:T(8,128)S(1)}, u32[]{:S(2)}, u32[]{:S(2)}) collective-permute-start(f32[2,8,8192]{2,1,0:T(8,128)S(1)} %fusion.7), channel_id=1, source_target_pairs={{0,256},{256,0},{32,288},{288,32},{64,320},{320,64},{96,352},{352,... | collective-permute-start | bytes 1572872 | tf_op jit(solution)/shard_map/ppermute | solution.py:18
  415.1 18.4 %collective-permute-done.8 = f32[2,8,8192]{2,1,0:T(8,128)S(1)} collective-permute-done((f32[2,8,8192]{2,1,0:T(8,128)S(1)}, f32[2,8,8192]{2,1,0:T(8,128)S(1)}, u32[]{:S(2)}, u32[]{:S(2)}) %collective-permute-start.8) | collective-permute-done | bytes 524320 | tf_op jit(solution)/shard_map/ppermute | solution.py:18
  433.7 0.1 reshape.427
  433.9 0.3 copy-done.2
  434.2 0.8 fusion.35
  435.0 70.1 %all-gather.3.cloned.1.call-done = bf16[32,4,8192]{2,1,0:T(4,128)(2,1)} async-done(((bf16[1,4,8192]{2,1,0:T(4,128)(2,1)}), bf16[32,4,8192]{2,1,0:T(4,128)(2,1)}) %all-gather.3.cloned.1.call-update) | async-done | bytes 2097168 | tf_op jit(solution)/shard_map/all_gather | solution.py:177
  505.1 2.5 reshape.429
  507.6 2.1 convolution_convert_fusion
  (45 shorter events, 3.3 us)
Async XLA Ops:
  6.5 501.1 %copy-start = (bf16[128,128]{1,0:T(8,128)(2,1)S(1)}, bf16[128,128]{1,0:T(8,128)(2,1)}, u32[]{:S(2)}) copy-start(bf16[128,128]{1,0:T(8,128)(2,1)} %param.9) | copy-start | bytes 98308
  6.5 9.0 %copy-start.1 = (f32[4,8192]{1,0:T(4,128)S(1)}, f32[4,8192]{1,0:T(4,128)}, u32[]{:S(2)}) copy-start(f32[4,8192]{1,0:T(4,128)} %param.7) | copy-start | bytes 393220
  6.5 498.5 %all-gather.3.cloned.1.call-start = ((), (), s32[]{:S(2)}) async-start(), calls=%async_computation | async-start | bytes 2162688 | tf_op jit(solution)/shard_map/all_gather | solution.py:177
  7.3 5.6 %collective-permute-start = (bf16[3,4,2]{2,1,0:T(4,128)(2,1)S(1)}, bf16[3,4,2]{2,1,0:T(4,128)(2,1)S(1)}, u32[]{:S(2)}, u32[]{:S(2)}) collective-permute-start(bf16[3,4,2]{2,1,0:T(4,128)(2,1)S(1)} %slice.150), channel_id=1, source_target_pairs={{0,32},{32,64},{64,96},{96,128},{128,160},{160,192},{192,224},{224... | collective-permute-start | bytes 152 | tf_op jit(solution)/shard_map/ppermute | solution.py:24
  15.8 61.0 %collective-permute-start.1 = (f32[2,16,8192]{2,1,0:T(8,128)S(1)}, f32[2,16,8192]{2,1,0:T(8,128)S(1)}, u32[]{:S(2)}, u32[]{:S(2)}) collective-permute-start(f32[2,16,8192]{2,1,0:T(8,128)S(1)} %select_maximum_fusion), channel_id=1, source_target_pairs={{0,256},{256,0},{32,288},{288,32},{64,320},{320,64},{96,352},{352,... | collective-permute-start | bytes 3145736 | tf_op jit(solution)/shard_map/ppermute | solution.py:18
  78.1 134.2 %collective-permute-start.2 = (f32[2,16,8192]{2,1,0:T(8,128)}, f32[2,16,8192]{2,1,0:T(8,128)S(1)}, u32[]{:S(2)}, u32[]{:S(2)}) collective-permute-start(f32[2,16,8192]{2,1,0:T(8,128)} %pad_maximum_fusion), channel_id=1, source_target_pairs={{0,128},{128,0},{32,160},{160,32},{64,192},{192,64},{96,224},{224,... | collective-permute-start | bytes 3145736 | tf_op jit(solution)/shard_map/ppermute | solution.py:18
  213.5 49.6 %collective-permute-start.3 = (f32[2,16,8192]{2,1,0:T(8,128)}, f32[2,16,8192]{2,1,0:T(8,128)S(1)}, u32[]{:S(2)}, u32[]{:S(2)}) collective-permute-start(f32[2,16,8192]{2,1,0:T(8,128)} %pad_maximum_fusion.1), channel_id=1, source_target_pairs={{0,64},{64,0},{32,96},{96,32},{128,192},{192,128},{160,224},{224,1... | collective-permute-start | bytes 3145736 | tf_op jit(solution)/shard_map/ppermute | solution.py:18
  264.4 26.3 %collective-permute-start.4 = (f32[2,16,8192]{2,1,0:T(8,128)}, f32[2,16,8192]{2,1,0:T(8,128)S(1)}, u32[]{:S(2)}, u32[]{:S(2)}) collective-permute-start(f32[2,16,8192]{2,1,0:T(8,128)} %pad_maximum_fusion.2), channel_id=1, source_target_pairs={{0,32},{32,0},{64,96},{96,64},{128,160},{160,128},{192,224},{224,1... | collective-permute-start | bytes 3145736 | tf_op jit(solution)/shard_map/ppermute | solution.py:18
  302.7 14.0 %collective-permute-start.5 = (f32[2,8,8192]{2,1,0:T(8,128)S(1)}, f32[2,8,8192]{2,1,0:T(8,128)S(1)}, u32[]{:S(2)}, u32[]{:S(2)}) collective-permute-start(f32[2,8,8192]{2,1,0:T(8,128)S(1)} %pad_maximum_fusion.3), channel_id=1, source_target_pairs={{0,32},{32,0},{64,96},{96,64},{128,160},{160,128},{192,224},{224,1... | collective-permute-start | bytes 1572872 | tf_op jit(solution)/shard_map/ppermute | solution.py:18
  316.9 27.5 %collective-permute-start.6 = (f32[2,8,8192]{2,1,0:T(8,128)S(1)}, f32[2,8,8192]{2,1,0:T(8,128)S(1)}, u32[]{:S(2)}, u32[]{:S(2)}) collective-permute-start(f32[2,8,8192]{2,1,0:T(8,128)S(1)} %fusion.5), channel_id=1, source_target_pairs={{0,64},{64,0},{32,96},{96,32},{128,192},{192,128},{160,224},{224,1... | collective-permute-start | bytes 1572872 | tf_op jit(solution)/shard_map/ppermute | solution.py:18
  344.6 63.4 %collective-permute-start.7 = (f32[2,8,8192]{2,1,0:T(8,128)S(1)}, f32[2,8,8192]{2,1,0:T(8,128)S(1)}, u32[]{:S(2)}, u32[]{:S(2)}) collective-permute-start(f32[2,8,8192]{2,1,0:T(8,128)S(1)} %fusion.6), channel_id=1, source_target_pairs={{0,128},{128,0},{32,160},{160,32},{64,192},{192,64},{96,224},{224,... | collective-permute-start | bytes 1572872 | tf_op jit(solution)/shard_map/ppermute | solution.py:18
  408.2 25.3 %collective-permute-start.8 = (f32[2,8,8192]{2,1,0:T(8,128)S(1)}, f32[2,8,8192]{2,1,0:T(8,128)S(1)}, u32[]{:S(2)}, u32[]{:S(2)}) collective-permute-start(f32[2,8,8192]{2,1,0:T(8,128)S(1)} %fusion.7), channel_id=1, source_target_pairs={{0,256},{256,0},{32,288},{288,32},{64,320},{320,64},{96,352},{352,... | collective-permute-start | bytes 1572872 | tf_op jit(solution)/shard_map/ppermute | solution.py:18
  433.6 0.7 copy-start.2
Sparse Core Ops, SparseCore 0:
  435.1 69.9 all-gather.2
where the time goes:
time: 517 us
  waiting for transfers between devices  386 us (75%)
  starting transfers between devices  88.3 us (17%)
  between operations  14.9 us (3%)
  matrix products  13 us (3%)
  other arithmetic  9.58 us (2%)
    ppermute x8, waiting for transfers between devices, partner_2(): return lax.ppermute(block, axis, route)  316 us
    ppermute x8, starting transfers between devices, partner_2(): return lax.ppermute(block, axis, route)  84 us
    all_gather x1, waiting for transfers between devices, shards(): lax.all_gather(gated_rows, 'chan', axis=0, tiled=True)  70.1 us
  transfers between devices with their start and end apart: 10, of which 9 were waited for; matrix products, arithmetic and copies ran while one was open for 0% of the time, Pallas kernels for 0%

commit v1 on v0

v1 whole, which is shorter than its diff:
```python
import math

import jax
import jax.numpy as jnp
import ml_dtypes
import numpy as np
from jax import lax
from jax.experimental import pallas as pl
from jax.experimental.pallas import tpu as pltpu
from jax.sharding import PartitionSpec as P

N1, N2 = 64, 128
BLOCK = N1 * N2
SLICES = 16
f32, bf16 = jnp.float32, jnp.bfloat16


def split_table(table):
    high = table.astype(ml_dtypes.bfloat16)
    low = (table - high.astype(np.float64)).astype(ml_dtypes.bfloat16)
    return high, low


def tables():
    row = np.arange(2 * N1)
    k1 = 4 * (row // 8) + row % 4
    imag = (row // 4) % 2 == 1
    n1, n2 = np.arange(N1), np.arange(N2)
    phase = 2 * math.pi * np.outer(k1 + 0.25, n1) / N1
    outer = np.where(imag[:, None], -np.sin(phase), np.cos(phase))
    oh, ol = split_table(outer)
    forward_outer = np.concatenate([oh, oh, ol], axis=1)
    ih, il = split_table(outer.T / BLOCK)
    inverse_outer = np.concatenate([ih, ih, il], axis=1)
    angle = 2 * math.pi * np.outer(k1 + 0.25, n2) / BLOCK
    turn_cos = np.cos(angle).astype(np.float32)
    turn_sin = np.where(imag[:, None], -np.sin(angle), np.sin(angle)).astype(np.float32)
    phase = 2 * math.pi * np.outer(n2, n2) / N2

    def inner(sign):
        high, low = split_table(np.concatenate([np.cos(phase), sign * np.sin(phase)], axis=1))
        return np.concatenate([high, high, low], axis=0)

    return forward_outer, inverse_outer, turn_cos, turn_sin, inner(-1.0), inner(1.0)


def halves_swapped(tile):
    rows = tile.shape[0]
    return pltpu.roll(tile.reshape(rows // 8, 8, N2), 4, 1).reshape(rows, N2)


def split(value):
    high = value.astype(bf16)
    return high, (value - high.astype(f32)).astype(bf16)


def imag_sign(rows):
    return jnp.where(lax.broadcasted_iota(jnp.int32, (rows, N2), 0) % 8 < 4, -1.0, 1.0).astype(f32)


def inner_stage(rows, table):
    high, low = split(rows)
    both = jnp.dot(jnp.concatenate([high, low, high], axis=1), table, preferred_element_type=f32)
    return both[:, :N2] + imag_sign(rows.shape[0]) * halves_swapped(both[:, N2:])


def short_filter(stream, edge, taps_ref, at):
    row = lax.broadcasted_iota(jnp.int32, (N1, N2), 0)
    lane = lax.broadcasted_iota(jnp.int32, (N1, N2), 1)
    total = taps_ref[3 * at] * stream
    edge = jnp.broadcast_to(edge, (8, N2))
    for lag in (1, 2):
        turned = pltpu.roll(stream, lag, 1)
        before = pltpu.roll(turned, 1, 0)
        first = jnp.concatenate([pltpu.roll(edge, lag, 1)] + [before[8:]], axis=0)
        before = jnp.where(row == 0, first, before)
        total = total + taps_ref[3 * at + lag] * jnp.where(lane < lag, before, turned)
    return total


def forward_kernel(feat_ref, edge_ref, taps_ref, filt_ref, outer_ref, cos_ref, sin_ref, inner_ref, out_ref):
    signals = []
    for c in range(4):
        mixed = [
            short_filter(feat_ref[i, c].astype(f32), edge_ref[4 * i + c : 4 * i + c + 1].astype(f32), taps_ref, 4 * i + c)
            for i in (1, 2)
        ]
        signals.append(mixed[0] * mixed[1])
    signals += [filt_ref[c] for c in range(4)]
    high, low = split(jnp.concatenate(signals, axis=1))
    stacked = jnp.concatenate([high, low, high], axis=0)
    first = jnp.dot(outer_ref[...], stacked, preferred_element_type=f32)
    for pair in range(4):
        done = []
        for s in (2 * pair, 2 * pair + 1):
            tile = first[:, N2 * s : N2 * (s + 1)]
            tile = tile * cos_ref[...] + halves_swapped(tile) * sin_ref[...]
            done.append(inner_stage(tile, inner_ref[...]).reshape(SLICES, 8, N2))
        out_ref[:, 16 * pair : 16 * pair + 16, :] = jnp.concatenate(done, axis=1).astype(bf16)


def gate_kernel(feat_ref, edge_ref, taps_ref, gain_ref, queries_ref, direct_ref):
    for c in range(4):
        mixed = [
            short_filter(feat_ref[i, c].astype(f32), edge_ref[4 * i + c : 4 * i + c + 1].astype(f32), taps_ref, 4 * i + c)
            for i in range(3)
        ]
        queries_ref[c] = mixed[0]
        direct_ref[c] = gain_ref[c] * (mixed[1] * mixed[2])


def mix_kernel(in_ref, out_ref):
    top = lax.broadcasted_iota(jnp.int32, (8, N2), 0) < 4
    for pair in range(2):
        sums = []
        for side in range(2):
            data, filt = [], []
            for block in range(SLICES):
                both = in_ref[block, 16 * pair : 16 * pair + 16, :].astype(f32)
                data.append(both[8 * side : 8 * side + 8])
                both = in_ref[block, 32 + 16 * pair : 48 + 16 * pair, :].astype(f32)
                filt.append(both[8 * side : 8 * side + 8])
            swapped = [pltpu.roll(tile, 4, 0) for tile in data]
            real_parts, imag_parts = [], []
            for m in range(SLICES):
                tile = filt[m]
                if m:
                    turned = pltpu.roll(filt[m - 1], 4, 0)
                    tile = tile + jnp.where(top, -turned, turned)
                turned = pltpu.roll(tile, 4, 0)
                real_parts.append(jnp.where(top, tile, turned))
                imag_parts.append(jnp.where(top, -turned, tile))
            row = []
            for d in range(SLICES):
                total = None
                for e in range(d + 1):
                    term = data[e] * real_parts[d - e] + swapped[e] * imag_parts[d - e]
                    total = term if total is None else total + term
                row.append(total)
            sums.append(row)
        for d in range(SLICES):
            out_ref[d, 16 * pair : 16 * pair + 16, :] = jnp.concatenate([sums[0][d], sums[1][d]], axis=0).astype(bf16)


def inverse_kernel(in_ref, queries_ref, direct_ref, outer_ref, cos_ref, sin_ref, inner_ref, out_ref):
    turned = []
    for pair in range(2):
        both = in_ref[:, 16 * pair : 16 * pair + 16, :].astype(f32)
        for side in range(2):
            tile = both[:, 8 * side : 8 * side + 8, :].reshape(2 * N1, N2)
            tile = inner_stage(tile, inner_ref[...])
            turned.append(tile * cos_ref[...] - halves_swapped(tile) * sin_ref[...])
    high, low = split(jnp.concatenate(turned, axis=1))
    stacked = jnp.concatenate([high, low, high], axis=0)
    convolved = jnp.dot(outer_ref[...], stacked, preferred_element_type=f32)
    for c in range(4):
        gated = queries_ref[c] * (convolved[:, N2 * c : N2 * (c + 1)] + direct_ref[c])
        gated = gated.astype(bf16)
        for copy in range(out_ref.shape[0]):
            out_ref[copy, N1 * c : N1 * (c + 1), :] = gated


vmem = pl.BlockSpec(memory_space=pltpu.VMEM)
smem = pl.BlockSpec(memory_space=pltpu.SMEM)


def call(kernel, specs, shape, dtype, *operands):
    if isinstance(shape, list):
        out_shape, out_specs = [jax.ShapeDtypeStruct(s, dtype) for s in shape], [vmem] * len(shape)
    else:
        out_shape, out_specs = jax.ShapeDtypeStruct(shape, dtype), vmem
    return pl.pallas_call(
        kernel,
        out_shape=out_shape,
        in_specs=specs,
        out_specs=out_specs,
        compiler_params=pltpu.CompilerParams(vmem_limit_bytes=32 << 20),
        cost_estimate=pl.CostEstimate(flops=1 << 24, bytes_accessed=1 << 20, transcendentals=0),
    )(*operands)


def gated_copies(features, short_taps, long_filter, skip_gain, copies):
    forward_outer, inverse_outer, turn_cos, turn_sin, forward_inner, inverse_inner = map(jnp.asarray, tables())
    seq = lax.axis_size("seq")
    edge = features[:, :, BLOCK - N2 :].reshape(12, N2)
    edge = lax.ppermute(edge, "seq", [(z, z + 1) for z in range(seq - 1)])
    feat = features.reshape(3, 4, N1, N2)
    taps = short_taps.reshape(36)
    spectra = call(
        forward_kernel,
        [vmem, vmem, smem, vmem, vmem, vmem, vmem, vmem],
        (SLICES, 64, N2),
        bf16,
        feat,
        edge,
        taps,
        long_filter.reshape(4, N1, N2),
        forward_outer,
        turn_cos,
        turn_sin,
        forward_inner,
    )
    spectra = lax.all_to_all(spectra, "seq", 0, 0, tiled=True)
    queries, direct = call(
        gate_kernel, [vmem, vmem, smem, smem], [(4, N1, N2)] * 2, f32, feat, edge, taps, skip_gain
    )
    mixed = call(mix_kernel, [vmem], (SLICES, 32, N2), bf16, spectra)
    mixed = lax.all_to_all(mixed, "seq", 0, 0, tiled=True)
    return call(
        inverse_kernel,
        [vmem] * 7,
        (copies, 4 * N1, N2),
        bf16,
        mixed,
        queries,
        direct,
        inverse_outer,
        turn_cos,
        turn_sin,
        inverse_inner,
    )


def shards(features, short_taps, long_filter, skip_gain, out_weight):
    chan = lax.axis_size("chan")
    chips = chan // 2
    sent = gated_copies(features, short_taps, long_filter, skip_gain, chips)
    same_core = [[2 * chip + core for chip in range(chips)] for core in range(2)]
    own = lax.all_to_all(sent, "chan", 0, 0, tiled=True, axis_index_groups=same_core)
    other = lax.ppermute(own, "chan", [(d, d ^ 1) for d in range(chan)])
    core = lax.axis_index("chan") % 2
    weight = out_weight.reshape(chips, 2, 4, N2)
    own_weight = lax.dynamic_index_in_dim(weight, core, 1, False).reshape(4 * chips, N2)
    other_weight = lax.dynamic_index_in_dim(weight, 1 - core, 1, False).reshape(4 * chips, N2)
    rows = jnp.concatenate([own.reshape(4 * chips, BLOCK), other.reshape(4 * chips, BLOCK)], axis=0)
    weight = jnp.concatenate([own_weight, other_weight], axis=0)
    projected = lax.dot_general(rows, weight, (((0,), (0,)), ((), ())), preferred_element_type=f32)
    return projected.astype(bf16)


def solution(mesh):
    placed = (
        P(None, "chan", "seq"),
        P(None, "chan", None),
        P("chan", "seq"),
        P("chan"),
        P(None, "chan"),
    )
    return jax.shard_map(
        shards, mesh=mesh, in_specs=placed, out_specs=P("seq", "chan"), check_vma=False
    )
```

time: 517 us -> 94.8 us (0.18)
  waiting for transfers between devices: 386 us -> 12.9 us
  starting transfers between devices: 88.3 us -> 21.5 us
  blocking collectives: 0 us -> 45.9 us
  between operations: 14.9 us -> 0.18 us
  matrix products: 13 us -> 2.07 us
  other arithmetic: 9.58 us -> 0 us
    ppermute x9 -> x2, waiting for transfers between devices: 316 us -> 1.71 us  [the longest x1 1.71 us: shards(): other = lax.ppermute(own, 'chan', [(d, d ^ 1) for d in range(chan)])]
    ppermute x9 -> x2, starting transfers between devices: 88.3 us -> 11.6 us  [the longest x1 7.25 us: shards(): other = lax.ppermute(own, 'chan', [(d, d ^ 1) for d in range(chan)])]
    all_gather x1 -> x0, waiting for transfers between devices: 70.1 us -> none  [shards(): lax.all_gather(gated_rows, 'chan', axis=0, tiled=True)]
    all_to_all x0 -> x2, blocking collectives: none -> 45.9 us  [the longest x1 26.6 us: gated_copies(): spectra = lax.all_to_all(spectra, 'seq', 0, 0, tiled=True)]
    all_to_all x0 -> x1, waiting for transfers between devices: none -> 11.2 us  [gated_copies(): mixed = lax.all_to_all(mixed, 'seq', 0, 0, tiled=True)]
    dot_general x17 -> x1, matrix products: 13 us -> 2.07 us  [shards(): lax.dot_general(rows, weight, (((0,), (0,)), ((), ())), preferred_element...]
    all_to_all x0 -> x1, starting transfers between devices: none -> 9.89 us  [gated_copies(): mixed = lax.all_to_all(mixed, 'seq', 0, 0, tiled=True)]
  transfers between devices with their start and end apart: 10 -> 3, of which waited for: 9 -> 2; matrix products, arithmetic and copies ran while one was open for 0% -> 4% of each run, Pallas kernels for 0% -> 1%
where the time goes in v1:
time: 94.8 us; the launch traced here: 94.2 us
  blocking collectives  45.9 us (48%)
  starting transfers between devices  21.5 us (23%)
  waiting for transfers between devices  12.9 us (14%)
  local copies, waits for them, and re-layouts  8.08 us (9%)
  Pallas kernels  3.62 us (4%)
  matrix products  2.07 us (2%)
    all_to_all x1, blocking collectives, gated_copies(): spectra = lax.all_to_all(spectra, 'seq', 0, 0, tiled=True)  26.6 us
    all_to_all x1, blocking collectives, shards(): lax.all_to_all(sent, 'chan', 0, 0, tiled=True, axis_index_groups=same_core)  19.3 us
    all_to_all x1, waiting for transfers between devices, gated_copies(): mixed = lax.all_to_all(mixed, 'seq', 0, 0, tiled=True)  11.2 us
    all_to_all x1, starting transfers between devices, gated_copies(): mixed = lax.all_to_all(mixed, 'seq', 0, 0, tiled=True)  9.89 us
    ppermute x1, starting transfers between devices, shards(): other = lax.ppermute(own, 'chan', [(d, d ^ 1) for d in range(chan)])  7.25 us
    unnamed x21, local copies, waits for them, and re-layouts  4.39 us
    ppermute x1, starting transfers between devices, gated_copies(): edge = lax.ppermute(edge, 'seq', [(z, z + 1) for z in range(seq - 1)])  4.36 us
    pallas_call x4, Pallas kernels, call(): pl.pallas_call(kernel, out_shape=out_shape, in_specs=specs, out_specs=out...  3.62 us
  transfers between devices with their start and end apart: 3, of which 2 were waited for; matrix products, arithmetic and copies ran while one was open for 4% of the time, Pallas kernels for 1%

profile of v1, /device:TPU:1, one launch (start us, length us, event | category | flops | bytes accessed | tf_op | source)
XLA Modules:
  0.0 94.2 jit_solution(1398230690476491471)
XLA Ops:
  0.0 0.0 copy-start.1
  0.0 0.0 copy-start.3
  0.0 0.0 copy-start.4
  0.0 0.0 copy-start.7
  0.0 0.0 copy-start.8
  0.0 0.8 slice.3
  0.8 4.4 %collective-permute-start = (bf16[12,128]{1,0:T(8,128)(2,1)S(1)}, bf16[12,128]{1,0:T(8,128)(2,1)S(1)}, u32[]{:S(2)}, u32[]{:S(2)}) collective-permute-start(bf16[12,128]{1,0:T(8,128)(2,1)S(1)} %reshape.30), channel_id=1, source_target_pairs={{0,32},{32,64},{64,96},{96,128},{128,160},{160,192},{192,224},{224... | collective-permute-start | bytes 9224 | tf_op jit(solution)/shard_map/ppermute | solution.py:186
  5.2 1.1 %reshape.29.feat_ref = bf16[3,4,64,128]{3,2,1,0:T(8,128)(2,1)S(1)} reshape(bf16[3,4,8192]{2,1,0:T(4,128)(2,1)} %param.11) | data formatting | bytes 393216 | tf_op jit(solution)/shard_map/reshape | solution.py:187
  6.3 0.8 reshape.31.taps_ref
  7.1 0.9 copy.14
  8.0 0.0 collective-permute-done.edge_ref
  8.0 0.0 copy-start
  8.1 0.8 copy-done
  8.9 0.0 copy-start.2
  8.9 0.8 copy-done.2
  9.7 0.0 copy-start.5
  9.7 0.9 copy-done.5
  10.7 0.0 copy-start.6
  10.7 0.8 copy-done.6
  11.5 1.3 %shard_map.109 = bf16[16,64,128]{2,1,0:T(8,128)(2,1)S(1)} custom-call(bf16[3,4,64,128]{3,2,1,0:T(8,128)(2,1)S(1)} %reshape.29.feat_ref, bf16[12,128]{1,0:T(8,128)(2,1)S(1)} %collective-permute-done.edge_ref, f32[36]{0:T(128)S(1)} %reshape.31.taps_ref, f32[4,64,128]{2,1,0:T(8,128)S(1)} %bitcast.7, bf16[128,192]{1,0:T(8,128)(2,1)S(1)} %copy-done.6, ...), custom_call_target="tpu_custom_call" | custom-call | flops 16777216 | bytes 1048576 | tf_op jit(solution)/shard_map/pallas_call | solution.py:172
  12.8 26.6 %all_to_all.15.in_ref = bf16[16,64,128]{2,1,0:T(8,128)(2,1)S(1)} all-to-all(bf16[16,64,128]{2,1,0:T(8,128)(2,1)S(1)} %shard_map.109), channel_id=1, replica_groups=mesh['seq'=16,'chan'=32] {'seq'}, dimensions={0} | all-to-all | bytes 524288 | tf_op jit(solution)/shard_map/all_to_all | solution.py:203
  39.4 1.1 %shard_map.110 = bf16[16,32,128]{2,1,0:T(8,128)(2,1)} custom-call(bf16[16,64,128]{2,1,0:T(8,128)(2,1)S(1)} %all_to_all.15.in_ref), custom_call_target="tpu_custom_call" | custom-call | flops 16777216 | bytes 1048576 | tf_op jit(solution)/shard_map/pallas_call | solution.py:172
  40.4 9.9 %all-to-all-start.1 = ((bf16[16,32,128]{2,1,0:T(8,128)(2,1)}), bf16[16,32,128]{2,1,0:T(8,128)(2,1)S(1)}, u32[]{:S(2)}, u32[]{:S(2)}) async-start(bf16[16,32,128]{2,1,0:T(8,128)(2,1)} %shard_map.110), calls=%async_computation.1 | async-start | bytes 262144 | tf_op jit(solution)/shard_map/all_to_all | solution.py:208
  50.3 0.0 copy-done.8
  50.4 0.0 copy-start.9
  50.4 0.8 shard_map.111
  51.2 11.2 %all-to-all-done.1.in_ref = bf16[16,32,128]{2,1,0:T(8,128)(2,1)S(1)} async-done(((bf16[16,32,128]{2,1,0:T(8,128)(2,1)}), bf16[16,32,128]{2,1,0:T(8,128)(2,1)S(1)}, u32[]{:S(2)}, u32[]{:S(2)}) %all-to-all-start.1) | async-done | bytes 131104 | tf_op jit(solution)/shard_map/all_to_all | solution.py:208
  62.3 0.0 copy-done.1
  62.4 0.0 copy-done.3
  62.4 0.0 copy-done.4
  62.4 0.0 copy-done.7
  62.4 0.5 shard_map.112
  62.9 19.3 %all_to_all.16 = bf16[16,256,128]{2,1,0:T(8,128)(2,1)S(1)} all-to-all(bf16[16,256,128]{2,1,0:T(8,128)(2,1)S(1)} %shard_map.112), channel_id=1, replica_groups={{0,2,4,6,8,10,12,14,16,18,20,22,24,26,28,30},{1,3,5,7,9,11,13,15,17,19,..., dimensions={0} | all-to-all | bytes 2097152 | tf_op jit(solution)/shard_map/all_to_all | solution.py:229
  82.2 7.3 %collective-permute-start.1 = (bf16[16,256,128]{2,1,0:T(8,128)(2,1)S(1)}, bf16[16,256,128]{2,1,0:T(8,128)(2,1)S(1)}, u32[]{:S(2)}, u32[]{:S(2)}) collective-permute-start(bf16[16,256,128]{2,1,0:T(8,128)(2,1)S(1)} %all_to_all.16), channel_id=1, source_target_pairs={{0,1},{1,0},{2,3},{3,2},{4,5},{5,4},{6,7},{7,6},{8,9},{9,8},{10,11... | collective-permute-start | bytes 3145736 | tf_op jit(solution)/shard_map/ppermute | solution.py:230
  89.4 0.0 copy-done.9
  89.5 0.5 reshape.33
  90.0 1.7 %collective-permute-done.1 = bf16[16,256,128]{2,1,0:T(8,128)(2,1)S(1)} collective-permute-done((bf16[16,256,128]{2,1,0:T(8,128)(2,1)S(1)}, bf16[16,256,128]{2,1,0:T(8,128)(2,1)S(1)}, u32[]{:S(2)}, u32[]{:S(2)}) %collective-permute-start.1) | collective-permute-done | bytes 1048608 | tf_op jit(solution)/shard_map/ppermute | solution.py:230
  91.7 0.5 reshape.34
  92.2 2.1 %convolution_convert_fusion = bf16[8192,128]{1,0:T(8,128)(2,1)} fusion(bf16[64,8192]{1,0:T(8,128)(2,1)S(1)} %reshape.34, bf16[64,8192]{1,0:T(8,128)(2,1)S(1)} %reshape.33, bf16[64,128]{1,0:T(8,128)(2,1)S(1)} %bitcast.10, bf16[64,128]{1,0:T(8,128)(2,1)S(1)} %bitcast.9), kind=kOutput, calls=%fused_computation | convolution fusion | flops 273743872 | bytes 4227072 | tf_op jit(solution)/shard_map/dot_general | solution.py:237
  (2 shorter events, 0.0 us)
Async XLA Ops:
  0.0 62.4 %copy-start.1 = (f32[128,128]{1,0:T(8,128)S(1)}, f32[128,128]{1,0:T(8,128)}, u32[]{:S(2)}) copy-start(f32[128,128]{1,0:T(8,128)} %constant.41.clone.sin_ref) | copy-start | bytes 196612
  0.0 62.4 %copy-start.3 = (f32[128,128]{1,0:T(8,128)S(1)}, f32[128,128]{1,0:T(8,128)}, u32[]{:S(2)}) copy-start(f32[128,128]{1,0:T(8,128)} %constant.40.clone.cos_ref) | copy-start | bytes 196612
  0.0 62.4 %copy-start.4 = (bf16[384,256]{1,0:T(8,128)(2,1)S(1)}, bf16[384,256]{1,0:T(8,128)(2,1)}, u32[]{:S(2)}) copy-start(bf16[384,256]{1,0:T(8,128)(2,1)} %constant.43.clone.inner_ref) | copy-start | bytes 589828
  0.0 62.4 %copy-start.7 = (bf16[64,384]{1,0:T(8,128)(2,1)S(1)}, bf16[64,384]{1,0:T(8,128)(2,1)}, u32[]{:S(2)}) copy-start(bf16[64,384]{1,0:T(8,128)(2,1)} %constant.39.clone.outer_ref) | copy-start | bytes 147460
  0.0 50.3 %copy-start.8 = (f32[4]{0:T(128)S(1)}, f32[4]{0:T(128)}, u32[]{:S(2)}) copy-start(f32[4]{0:T(128)} %gain_ref.1) | copy-start | bytes 52
  0.8 7.2 %collective-permute-start = (bf16[12,128]{1,0:T(8,128)(2,1)S(1)}, bf16[12,128]{1,0:T(8,128)(2,1)S(1)}, u32[]{:S(2)}, u32[]{:S(2)}) collective-permute-start(bf16[12,128]{1,0:T(8,128)(2,1)S(1)} %reshape.30), channel_id=1, source_target_pairs={{0,32},{32,64},{64,96},{96,128},{128,160},{160,192},{192,224},{224... | collective-permute-start | bytes 9224 | tf_op jit(solution)/shard_map/ppermute | solution.py:186
  8.0 0.8 copy-start
  8.9 0.8 copy-start.2
  9.7 0.9 copy-start.5
  10.7 0.8 copy-start.6
  40.4 21.9 %all-to-all-start.1 = ((bf16[16,32,128]{2,1,0:T(8,128)(2,1)}), bf16[16,32,128]{2,1,0:T(8,128)(2,1)S(1)}, u32[]{:S(2)}, u32[]{:S(2)}) async-start(bf16[16,32,128]{2,1,0:T(8,128)(2,1)} %shard_map.110), calls=%async_computation.1 | async-start | bytes 262144 | tf_op jit(solution)/shard_map/all_to_all | solution.py:208
  50.4 39.1 %copy-start.9 = (bf16[128,128]{1,0:T(8,128)(2,1)S(1)}, bf16[128,128]{1,0:T(8,128)(2,1)}, u32[]{:S(2)}) copy-start(bf16[128,128]{1,0:T(8,128)(2,1)} %param.15) | copy-start | bytes 98308
  82.2 9.5 %collective-permute-start.1 = (bf16[16,256,128]{2,1,0:T(8,128)(2,1)S(1)}, bf16[16,256,128]{2,1,0:T(8,128)(2,1)S(1)}, u32[]{:S(2)}, u32[]{:S(2)}) collective-permute-start(bf16[16,256,128]{2,1,0:T(8,128)(2,1)S(1)} %all_to_all.16), channel_id=1, source_target_pairs={{0,1},{1,0},{2,3},{3,2},{4,5},{5,4},{6,7},{7,6},{8,9},{9,8},{10,11... | collective-permute-start | bytes 3145736 | tf_op jit(solution)/shard_map/ppermute | solution.py:230

commit v2 on v1

--- a/solution.py
+++ b/solution.py
@@ -64,31 +64,53 @@
     return both[:, :N2] + imag_sign(rows.shape[0]) * halves_swapped(both[:, N2:])
 
 
-def short_filter(stream, edge, taps_ref, at):
-    row = lax.broadcasted_iota(jnp.int32, (N1, N2), 0)
-    lane = lax.broadcasted_iota(jnp.int32, (N1, N2), 1)
-    total = taps_ref[3 * at] * stream
-    edge = jnp.broadcast_to(edge, (8, N2))
+def lane_index(shape):
+    return lax.broadcasted_iota(jnp.int32, shape, 1)
+
+
+def short_filter(stream, taps, edge=None):
+    total = taps[:, 0:1] * stream
     for lag in (1, 2):
         turned = pltpu.roll(stream, lag, 1)
-        before = pltpu.roll(turned, 1, 0)
-        first = jnp.concatenate([pltpu.roll(edge, lag, 1)] + [before[8:]], axis=0)
-        before = jnp.where(row == 0, first, before)
-        total = total + taps_ref[3 * at + lag] * jnp.where(lane < lag, before, turned)
+        head = turned[:, :N2]
+        before = jnp.zeros_like(head) if edge is None else pltpu.roll(edge, lag, 1)
+        head = jnp.where(lane_index(head.shape) < lag, before, head)
+        total = total + taps[:, lag : lag + 1] * jnp.concatenate([head, turned[:, N2:]], axis=1)
     return total
 
 
-def forward_kernel(feat_ref, edge_ref, taps_ref, filt_ref, outer_ref, cos_ref, sin_ref, inner_ref, out_ref):
-    signals = []
-    for c in range(4):
-        mixed = [
-            short_filter(feat_ref[i, c].astype(f32), edge_ref[4 * i + c : 4 * i + c + 1].astype(f32), taps_ref, 4 * i + c)
-            for i in (1, 2)
-        ]
-        signals.append(mixed[0] * mixed[1])
-    signals += [filt_ref[c] for c in range(4)]
+def to_blocks(upper, lower, rows_ref):
+    both = jnp.concatenate([upper, lower], axis=0)
+    for n1 in range(N1):
+        rows_ref[8 * n1 : 8 * n1 + 8, :] = both[:, N2 * n1 : N2 * (n1 + 1)]
+    return [rows_ref[pl.ds(s, N1, stride=8), :] for s in range(8)]
+
+
+def forward_kernel(
+    feat_hbm, taps_hbm, filt_hbm, outer_hbm, cos_hbm, sin_hbm, inner_hbm, out_ref,
+    feat_ref, taps_ref, filt_ref, outer_ref, cos_ref, sin_ref, inner_ref, rows_ref, sems,
+):
+    sources = (feat_hbm, taps_hbm, filt_hbm, outer_hbm, cos_hbm, sin_hbm, inner_hbm)
+    places = (feat_ref, taps_ref, filt_ref, outer_ref, cos_ref, sin_ref, inner_ref)
+    copies = [pltpu.make_async_copy(s, d, sems.at[n]) for n, (s, d) in enumerate(zip(sources, places))]
+    for copy in copies:
+        copy.start()
+    for copy in copies[:2]:
+        copy.wait()
+    streams = [feat_ref[i].astype(f32) for i in range(3)]
+    ends = [
+        jnp.where(lane_index((4, N2)) < N1, stream[:, :N2], stream[:, BLOCK - N2 :]) for stream in streams
+    ]
+    ends = jnp.concatenate(ends + [jnp.zeros((4, N2), f32)], axis=0).astype(bf16)
+    for device in range(SLICES):
+        out_ref[device, 64:80, :] = ends
+    product = short_filter(streams[1], taps_ref[1]) * short_filter(streams[2], taps_ref[2])
+    copies[2].wait()
+    signals = to_blocks(product, filt_ref[...], rows_ref)
     high, low = split(jnp.concatenate(signals, axis=1))
     stacked = jnp.concatenate([high, low, high], axis=0)
+    for copy in copies[3:]:
+        copy.wait()
     first = jnp.dot(outer_ref[...], stacked, preferred_element_type=f32)
     for pair in range(4):
         done = []
@@ -99,25 +121,63 @@
         out_ref[:, 16 * pair : 16 * pair + 16, :] = jnp.concatenate(done, axis=1).astype(bf16)
 
 
-def gate_kernel(feat_ref, edge_ref, taps_ref, gain_ref, queries_ref, direct_ref):
+def gate_kernel(
+    feat_hbm, taps_hbm, spectra_hbm, gain_ref, queries_ref, direct_ref, feat_ref, taps_ref, ends_ref, rows_ref, sems
+):
+    device = lax.axis_index("seq")
+    ends = spectra_hbm.at[jnp.maximum(device - 1, 0), pl.ds(64, 16), :]
+    copies = [
+        pltpu.make_async_copy(s, d, sems.at[n])
+        for n, (s, d) in enumerate(((feat_hbm, feat_ref), (taps_hbm, taps_ref), (ends, ends_ref)))
+    ]
+    for copy in copies:
+        copy.start()
+    for copy in copies:
+        copy.wait()
+    edges = jnp.where(device > 0, ends_ref[...].astype(f32), 0.0)
+    mixed = [
+        short_filter(feat_ref[i].astype(f32), taps_ref[i], edges[4 * i : 4 * i + 4]) for i in range(3)
+    ]
+    rows = to_blocks(mixed[0], mixed[1] * mixed[2], rows_ref)
     for c in range(4):
-        mixed = [
-            short_filter(feat_ref[i, c].astype(f32), edge_ref[4 * i + c : 4 * i + c + 1].astype(f32), taps_ref, 4 * i + c)
-            for i in range(3)
-        ]
-        queries_ref[c] = mixed[0]
-        direct_ref[c] = gain_ref[c] * (mixed[1] * mixed[2])
-
-
-def mix_kernel(in_ref, out_ref):
+        queries_ref[c] = rows[c]
+        direct_ref[c] = gain_ref[c] * rows[4 + c]
+
+
+def edge_terms(in_ref, taps_ref):
+    lane = lane_index((16, N2))
+    ends = [in_ref[block, 64:80, :].astype(f32) for block in range(SLICES)]
+    taps = jnp.concatenate([taps_ref[0], taps_ref[1], taps_ref[2], taps_ref[2]], axis=0)
+    taps = [jnp.broadcast_to(taps[:, k : k + 1], (16, N2)) for k in range(3)]
+
+    def products(tokens):
+        mixed = taps[2] * tokens + taps[1] * pltpu.roll(tokens, N2 - 1, 1) + taps[0] * pltpu.roll(tokens, N2 - 2, 1)
+        return mixed * pltpu.roll(mixed, 12, 0)
+
+    missing = [None]
+    for block in range(1, SLICES):
+        own = pltpu.roll(ends[block], 2, 1)
+        whole = jnp.where(lane < 2, pltpu.roll(ends[block - 1], 2, 1), own)
+        missing.append(products(whole) - products(jnp.where(lane < 2, 0.0, own)))
+    return missing
+
+
+def mix_kernel(in_ref, taps_ref, wave_ref, out_ref):
     top = lax.broadcasted_iota(jnp.int32, (8, N2), 0) < 4
+    missing = edge_terms(in_ref, taps_ref)
+    wave = wave_ref[lax.axis_index("seq")]
     for pair in range(2):
         sums = []
         for side in range(2):
+            row = 4 + 2 * pair + side
             data, filt = [], []
             for block in range(SLICES):
                 both = in_ref[block, 16 * pair : 16 * pair + 16, :].astype(f32)
-                data.append(both[8 * side : 8 * side + 8])
+                tile = both[8 * side : 8 * side + 8]
+                if block:
+                    lack = missing[block][row : row + 1]
+                    tile = tile + jnp.where(top, lack[:, 0:1], 0.0) + lack[:, 1:2] * wave
+                data.append(tile)
                 both = in_ref[block, 32 + 16 * pair : 48 + 16 * pair, :].astype(f32)
                 filt.append(both[8 * side : 8 * side + 8])
             swapped = [pltpu.roll(tile, 4, 0) for tile in data]
@@ -160,11 +220,20 @@
             out_ref[copy, N1 * c : N1 * (c + 1), :] = gated
 
 
+def wave_table():
+    row = np.arange(2 * N1)
+    k1 = 4 * (row // 8) + row % 4
+    angle = 2 * math.pi * (k1[:, None] + 64 * np.arange(N2)[None, :] + 0.25) / BLOCK
+    imag = (row // 4) % 2 == 1
+    return np.where(imag[:, None], -np.sin(angle), np.cos(angle)).astype(np.float32).reshape(SLICES, 8, N2)
+
+
 vmem = pl.BlockSpec(memory_space=pltpu.VMEM)
 smem = pl.BlockSpec(memory_space=pltpu.SMEM)
-
-
-def call(kernel, specs, shape, dtype, *operands):
+anywhere = pl.BlockSpec(memory_space=pl.ANY)
+
+
+def call(kernel, specs, shape, dtype, *operands, scratch=()):
     if isinstance(shape, list):
         out_shape, out_specs = [jax.ShapeDtypeStruct(s, dtype) for s in shape], [vmem] * len(shape)
     else:
@@ -174,6 +243,7 @@
         out_shape=out_shape,
         in_specs=specs,
         out_specs=out_specs,
+        scratch_shapes=scratch,
         compiler_params=pltpu.CompilerParams(vmem_limit_bytes=32 << 20),
         cost_estimate=pl.CostEstimate(flops=1 << 24, bytes_accessed=1 << 20, transcendentals=0),
     )(*operands)
@@ -181,30 +251,37 @@
 
 def gated_copies(features, short_taps, long_filter, skip_gain, copies):
     forward_outer, inverse_outer, turn_cos, turn_sin, forward_inner, inverse_inner = map(jnp.asarray, tables())
-    seq = lax.axis_size("seq")
-    edge = features[:, :, BLOCK - N2 :].reshape(12, N2)
-    edge = lax.ppermute(edge, "seq", [(z, z + 1) for z in range(seq - 1)])
-    feat = features.reshape(3, 4, N1, N2)
-    taps = short_taps.reshape(36)
+    held = (features, short_taps, long_filter, forward_outer, turn_cos, turn_sin, forward_inner)
+    rows = pltpu.VMEM((8 * N1, N2), f32)
     spectra = call(
         forward_kernel,
-        [vmem, vmem, smem, vmem, vmem, vmem, vmem, vmem],
-        (SLICES, 64, N2),
+        [anywhere] * 7,
+        (SLICES, 80, N2),
         bf16,
-        feat,
-        edge,
-        taps,
-        long_filter.reshape(4, N1, N2),
-        forward_outer,
-        turn_cos,
-        turn_sin,
-        forward_inner,
+        *held,
+        scratch=[pltpu.VMEM(x.shape, x.dtype) for x in held] + [rows, pltpu.SemaphoreType.DMA((7,))],
     )
     spectra = lax.all_to_all(spectra, "seq", 0, 0, tiled=True)
     queries, direct = call(
-        gate_kernel, [vmem, vmem, smem, smem], [(4, N1, N2)] * 2, f32, feat, edge, taps, skip_gain
-    )
-    mixed = call(mix_kernel, [vmem], (SLICES, 32, N2), bf16, spectra)
+        gate_kernel,
+        [anywhere] * 3 + [smem],
+        [(4, N1, N2)] * 2,
+        f32,
+        features,
+        short_taps,
+        spectra,
+        skip_gain,
+        scratch=[
+            pltpu.VMEM(features.shape, bf16),
+            pltpu.VMEM(short_taps.shape, f32),
+            pltpu.VMEM((16, N2), bf16),
+            rows,
+            pltpu.SemaphoreType.DMA((3,)),
+        ],
+    )
+    mixed = call(
+        mix_kernel, [vmem] * 3, (SLICES, 32, N2), bf16, spectra, short_taps, jnp.asarray(wave_table())
+    )
     mixed = lax.all_to_all(mixed, "seq", 0, 0, tiled=True)
     return call(
         inverse_kernel,

time: 94.8 us -> 97 us (1.023)
  blocking collectives: 45.9 us -> 50.5 us
  starting transfers between devices: 21.5 us -> 18.4 us
  Pallas kernels: 3.62 us -> 5.23 us
    ppermute x1 -> x0, starting transfers between devices: 4.36 us -> none  [gated_copies(): edge = lax.ppermute(edge, 'seq', [(z, z + 1) for z in range(seq - 1)])]
    all_to_all x1, blocking collectives: 26.6 us -> 30.8 us  [gated_copies(): spectra = lax.all_to_all(spectra, 'seq', 0, 0, tiled=True)]
    unnamed x21 -> x32, local copies, waits for them, and re-layouts: 4.39 us -> 6.85 us
    reshape x3 -> x0, local copies, waits for them, and re-layouts: 1.95 us -> none  [the longest x1 1.15 us: gated_copies(): feat = features.reshape(3, 4, N1, N2)]
    all_to_all x1, starting transfers between devices: 9.89 us -> 11.6 us  [gated_copies(): mixed = lax.all_to_all(mixed, 'seq', 0, 0, tiled=True)]
    pallas_call x4, Pallas kernels: 3.62 us -> 5.23 us  [call(): pl.pallas_call(kernel, out_shape=out_shape, in_specs=specs, out_specs=out...]
  transfers between devices with their start and end apart: 3 -> 2, of which waited for: 2 -> 2; matrix products, arithmetic and copies ran while one was open for 4% -> 1% of each run, Pallas kernels for 1% -> 1%
where the time goes in v2:
time: 97 us; the launch traced here: 96.4 us
  blocking collectives  50.5 us (52%)
  starting transfers between devices  18.4 us (19%)
  waiting for transfers between devices  12.3 us (13%)
  local copies, waits for them, and re-layouts  7.84 us (8%)
  Pallas kernels  5.23 us (5%)
  matrix products  2.07 us (2%)
    all_to_all x1, blocking collectives, gated_copies(): spectra = lax.all_to_all(spectra, 'seq', 0, 0, tiled=True)  30.8 us
    all_to_all x1, blocking collectives, shards(): lax.all_to_all(sent, 'chan', 0, 0, tiled=True, axis_index_groups=same_core)  19.7 us
    all_to_all x1, starting transfers between devices, gated_copies(): mixed = lax.all_to_all(mixed, 'seq', 0, 0, tiled=True)  11.6 us
    all_to_all x1, waiting for transfers between devices, gated_copies(): mixed = lax.all_to_all(mixed, 'seq', 0, 0, tiled=True)  10.6 us
    unnamed x32, local copies, waits for them, and re-layouts  6.85 us
    ppermute x1, starting transfers between devices, shards(): other = lax.ppermute(own, 'chan', [(d, d ^ 1) for d in range(chan)])  6.77 us
    pallas_call x4, Pallas kernels, call(): pl.pallas_call(kernel, out_shape=out_shape, in_specs=specs, out_specs=out...  5.23 us
    dot_general x1, matrix products, shards(): lax.dot_general(rows, weight, (((0,), (0,)), ((), ())), preferred_element...  2.07 us
  transfers between devices with their start and end apart: 2, of which 2 were waited for; matrix products, arithmetic and copies ran while one was open for 1% of the time, Pallas kernels for 1%

profile of v2, /device:TPU:1, one launch (start us, length us, event | category | flops | bytes accessed | tf_op | source)
XLA Modules:
  0.0 96.4 jit_solution(4899954567486627947)
XLA Ops:
  0.0 0.0 copy-start
  0.0 0.9 copy-done
  0.9 0.0 copy-start.2
  0.9 0.8 copy-done.2
  1.8 0.0 copy-start.4
  1.8 0.8 copy-done.4
  2.6 0.0 copy-start.7
  2.6 0.9 copy-done.7
  3.5 0.0 copy-start.8
  3.5 0.9 copy-done.8
  4.4 0.0 copy-start.9
  4.4 0.8 copy-done.9
  5.3 0.0 copy-start.11
  5.3 0.7 copy-done.11
  6.0 0.0 copy-start.1
  6.0 0.0 copy-start.12
  6.0 0.0 copy-start.14
  6.0 0.0 copy-start.3
  6.0 0.0 copy-start.5
  6.0 0.0 copy-start.6
  6.0 0.0 copy-start.13
  6.0 2.0 %shard_map.118 = bf16[16,80,128]{2,1,0:T(8,128)(2,1)S(1)} custom-call(bf16[3,4,8192]{2,1,0:T(4,128)(2,1)S(1)} %copy-done, f32[3,4,3]{2,1,0:T(4,128)S(1)} %copy-done.11, f32[4,8192]{1,0:T(4,128)S(1)} %copy-done.8, bf16[128,192]{1,0:T(8,128)(2,1)S(1)} %copy-done.9, f32[128,128]{1,0:T(8,128)S(1)} %copy-done.4, f32[128,128]{1,0:T(8,128)S(1)} %copy-done.2, ...), custom_call_target="tpu_custom_call" | custom-call | flops 16777216 | bytes 1048576 | tf_op jit(solution)/shard_map/pallas_call | solution.py:241
  8.0 30.8 %all_to_all.15.in_ref.spectra_hbm = bf16[16,80,128]{2,1,0:T(8,128)(2,1)S(1)} all-to-all(bf16[16,80,128]{2,1,0:T(8,128)(2,1)S(1)} %shard_map.118), channel_id=1, replica_groups=mesh['seq'=16,'chan'=32] {'seq'}, dimensions={0} | all-to-all | bytes 655360 | tf_op jit(solution)/shard_map/all_to_all | solution.py:264
  38.8 0.0 copy-start.10
  38.8 0.8 copy-done.10
  39.6 1.4 %shard_map.119 = bf16[16,32,128]{2,1,0:T(8,128)(2,1)} custom-call(bf16[16,80,128]{2,1,0:T(8,128)(2,1)S(1)} %all_to_all.15.in_ref.spectra_hbm, f32[3,4,3]{2,1,0:T(4,128)S(1)} %copy-done.11, f32[16,8,128]{2,1,0:T(8,128)S(1)} %copy-done.10), custom_call_target="tpu_custom_call" | custom-call | flops 16777216 | bytes 1048576 | tf_op jit(solution)/shard_map/pallas_call | solution.py:241
  41.0 11.6 %all-to-all-start.1 = ((bf16[16,32,128]{2,1,0:T(8,128)(2,1)}), bf16[16,32,128]{2,1,0:T(8,128)(2,1)S(1)}, u32[]{:S(2)}, u32[]{:S(2)}) async-start(bf16[16,32,128]{2,1,0:T(8,128)(2,1)} %shard_map.119), calls=%async_computation.1 | async-start | bytes 262144 | tf_op jit(solution)/shard_map/all_to_all | solution.py:285
  52.6 0.0 copy-done.1
  52.6 0.0 copy-done.12
  52.6 0.0 copy-done.14
  52.6 1.4 %shard_map.120 = (f32[4,64,128]{2,1,0:T(8,128)S(1)}, f32[4,64,128]{2,1,0:T(8,128)S(1)}) custom-call(bf16[3,4,8192]{2,1,0:T(4,128)(2,1)S(1)} %copy-done.1, f32[3,4,3]{2,1,0:T(4,128)S(1)} %copy-done.12, bf16[16,80,128]{2,1,0:T(8,128)(2,1)S(1)} %all_to_all.15.in_ref.spectra_hbm, f32[4]{0:T(128)S(1)} %copy-done.14), custom_call_target="tpu_custom_call" | custom-call | flops 16777216 | bytes 1048576 | tf_op jit(solution)/shard_map/pallas_call | solution.py:241
  54.0 0.0 copy-start.15
  54.0 10.6 %all-to-all-done.1.in_ref = bf16[16,32,128]{2,1,0:T(8,128)(2,1)S(1)} async-done(((bf16[16,32,128]{2,1,0:T(8,128)(2,1)}), bf16[16,32,128]{2,1,0:T(8,128)(2,1)S(1)}, u32[]{:S(2)}, u32[]{:S(2)}) %all-to-all-start.1) | async-done | bytes 131104 | tf_op jit(solution)/shard_map/all_to_all | solution.py:285
  64.5 0.0 copy-done.3
  64.5 0.0 copy-done.5
  64.5 0.0 copy-done.6
  64.6 0.0 copy-done.13
  64.6 0.5 shard_map.121
  65.1 19.7 %all_to_all.16 = bf16[16,256,128]{2,1,0:T(8,128)(2,1)S(1)} all-to-all(bf16[16,256,128]{2,1,0:T(8,128)(2,1)S(1)} %shard_map.121), channel_id=1, replica_groups={{0,2,4,6,8,10,12,14,16,18,20,22,24,26,28,30},{1,3,5,7,9,11,13,15,17,19,..., dimensions={0} | all-to-all | bytes 2097152 | tf_op jit(solution)/shard_map/all_to_all | solution.py:306
  84.8 6.8 %collective-permute-start = (bf16[16,256,128]{2,1,0:T(8,128)(2,1)S(1)}, bf16[16,256,128]{2,1,0:T(8,128)(2,1)S(1)}, u32[]{:S(2)}, u32[]{:S(2)}) collective-permute-start(bf16[16,256,128]{2,1,0:T(8,128)(2,1)S(1)} %all_to_all.16), channel_id=1, source_target_pairs={{0,1},{1,0},{2,3},{3,2},{4,5},{5,4},{6,7},{7,6},{8,9},{9,8},{10,11... | collective-permute-start | bytes 3145736 | tf_op jit(solution)/shard_map/ppermute | solution.py:307
  91.6 0.0 copy-done.15
  91.7 0.5 reshape.17
  92.2 1.7 %collective-permute-done = bf16[16,256,128]{2,1,0:T(8,128)(2,1)S(1)} collective-permute-done((bf16[16,256,128]{2,1,0:T(8,128)(2,1)S(1)}, bf16[16,256,128]{2,1,0:T(8,128)(2,1)S(1)}, u32[]{:S(2)}, u32[]{:S(2)}) %collective-permute-start) | collective-permute-done | bytes 1048608 | tf_op jit(solution)/shard_map/ppermute | solution.py:307
  93.9 0.5 reshape.18
  94.4 2.1 %convolution_convert_fusion = bf16[8192,128]{1,0:T(8,128)(2,1)} fusion(bf16[64,8192]{1,0:T(8,128)(2,1)S(1)} %reshape.18, bf16[64,8192]{1,0:T(8,128)(2,1)S(1)} %reshape.17, bf16[64,128]{1,0:T(8,128)(2,1)S(1)} %bitcast.4, bf16[64,128]{1,0:T(8,128)(2,1)S(1)} %bitcast.3), kind=kOutput, calls=%fused_computation | convolution fusion | flops 273743872 | bytes 4227072 | tf_op jit(solution)/shard_map/dot_general | solution.py:314
  (1 shorter events, 0.0 us)
Async XLA Ops:
  0.0 0.9 copy-start
  0.9 0.8 copy-start.2
  1.8 0.8 copy-start.4
  2.6 0.9 copy-start.7
  3.5 0.9 copy-start.8
  4.4 0.8 copy-start.9
  5.3 0.7 copy-start.11
  6.0 46.6 %copy-start.1 = (bf16[3,4,8192]{2,1,0:T(4,128)(2,1)S(1)}, bf16[3,4,8192]{2,1,0:T(4,128)(2,1)}, u32[]{:S(2)}) copy-start(bf16[3,4,8192]{2,1,0:T(4,128)(2,1)} %feat_hbm.3) | copy-start | bytes 589828
  6.0 46.6 %copy-start.12 = (f32[3,4,3]{2,1,0:T(4,128)S(1)}, f32[3,4,3]{2,1,0:T(4,128)}, u32[]{:S(2)}) copy-start(f32[3,4,3]{2,1,0:T(4,128)} %taps_hbm.3) | copy-start | bytes 436
  6.0 46.6 %copy-start.14 = (f32[4]{0:T(128)S(1)}, f32[4]{0:T(128)}, u32[]{:S(2)}) copy-start(f32[4]{0:T(128)} %gain_ref.1) | copy-start | bytes 52
  6.0 58.6 %copy-start.3 = (f32[128,128]{1,0:T(8,128)S(1)}, f32[128,128]{1,0:T(8,128)}, u32[]{:S(2)}) copy-start(f32[128,128]{1,0:T(8,128)} %constant.43.clone.sin_hbm.sin_ref) | copy-start | bytes 196612
  6.0 58.6 %copy-start.5 = (f32[128,128]{1,0:T(8,128)S(1)}, f32[128,128]{1,0:T(8,128)}, u32[]{:S(2)}) copy-start(f32[128,128]{1,0:T(8,128)} %constant.42.clone.cos_hbm.cos_ref) | copy-start | bytes 196612
  6.0 58.6 %copy-start.6 = (bf16[384,256]{1,0:T(8,128)(2,1)S(1)}, bf16[384,256]{1,0:T(8,128)(2,1)}, u32[]{:S(2)}) copy-start(bf16[384,256]{1,0:T(8,128)(2,1)} %constant.45.clone.inner_ref) | copy-start | bytes 589828
  6.0 58.5 %copy-start.13 = (bf16[64,384]{1,0:T(8,128)(2,1)S(1)}, bf16[64,384]{1,0:T(8,128)(2,1)}, u32[]{:S(2)}) copy-start(bf16[64,384]{1,0:T(8,128)(2,1)} %constant.41.clone.outer_ref) | copy-start | bytes 147460
  38.8 0.8 copy-start.10
  41.0 23.6 %all-to-all-start.1 = ((bf16[16,32,128]{2,1,0:T(8,128)(2,1)}), bf16[16,32,128]{2,1,0:T(8,128)(2,1)S(1)}, u32[]{:S(2)}, u32[]{:S(2)}) async-start(bf16[16,32,128]{2,1,0:T(8,128)(2,1)} %shard_map.119), calls=%async_computation.1 | async-start | bytes 262144 | tf_op jit(solution)/shard_map/all_to_all | solution.py:285
  54.0 37.7 %copy-start.15 = (bf16[128,128]{1,0:T(8,128)(2,1)S(1)}, bf16[128,128]{1,0:T(8,128)(2,1)}, u32[]{:S(2)}) copy-start(bf16[128,128]{1,0:T(8,128)(2,1)} %param.16) | copy-start | bytes 98308
  84.8 9.0 %collective-permute-start = (bf16[16,256,128]{2,1,0:T(8,128)(2,1)S(1)}, bf16[16,256,128]{2,1,0:T(8,128)(2,1)S(1)}, u32[]{:S(2)}, u32[]{:S(2)}) collective-permute-start(bf16[16,256,128]{2,1,0:T(8,128)(2,1)S(1)} %all_to_all.16), channel_id=1, source_target_pairs={{0,1},{1,0},{2,3},{3,2},{4,5},{5,4},{6,7},{7,6},{8,9},{9,8},{10,11... | collective-permute-start | bytes 3145736 | tf_op jit(solution)/shard_map/ppermute | solution.py:307

commit v3 on v2

--- a/solution.py
+++ b/solution.py
@@ -86,6 +86,20 @@
     return [rows_ref[pl.ds(s, N1, stride=8), :] for s in range(8)]
 
 
+def block_ends(streams, taps_ref):
+    lane = lane_index((8, N2))
+    first = jnp.concatenate([stream[:, :N2] for stream in streams[1:]], axis=0)
+    last = jnp.concatenate([stream[:, BLOCK - N2 :] for stream in streams[1:]], axis=0)
+    query = jnp.concatenate([streams[0][:, BLOCK - N2 :]] * 2, axis=0)
+    taps = jnp.concatenate([taps_ref[1], taps_ref[2]], axis=0)
+    own = taps[:, 0:1] * first + jnp.where(lane == 1, taps[:, 1:2] * pltpu.roll(first, 1, 1), 0.0)
+    given = taps[:, 2:3] * last + jnp.where(lane == N2 - 2, taps[:, 1:2] * pltpu.roll(last, N2 - 1, 1), 0.0)
+    exact = jnp.where(lane < 2, own, pltpu.roll(given, 4, 1))
+    rest = exact - exact.astype(bf16).astype(f32)
+    rest = jnp.where(lane < N1 + 4, pltpu.roll(rest, N1, 1), jnp.where(lane < N2 - 2, pltpu.roll(query, N2 - 2, 1), last))
+    return jnp.where(lane < 4, exact, rest)
+
+
 def forward_kernel(
     feat_hbm, taps_hbm, filt_hbm, outer_hbm, cos_hbm, sin_hbm, inner_hbm, out_ref,
     feat_ref, taps_ref, filt_ref, outer_ref, cos_ref, sin_ref, inner_ref, rows_ref, sems,
@@ -98,12 +112,9 @@
     for copy in copies[:2]:
         copy.wait()
     streams = [feat_ref[i].astype(f32) for i in range(3)]
-    ends = [
-        jnp.where(lane_index((4, N2)) < N1, stream[:, :N2], stream[:, BLOCK - N2 :]) for stream in streams
-    ]
-    ends = jnp.concatenate(ends + [jnp.zeros((4, N2), f32)], axis=0).astype(bf16)
+    ends = block_ends(streams, taps_ref).astype(bf16)
     for device in range(SLICES):
-        out_ref[device, 64:80, :] = ends
+        out_ref[device, 64:72, :] = ends
     product = short_filter(streams[1], taps_ref[1]) * short_filter(streams[2], taps_ref[2])
     copies[2].wait()
     signals = to_blocks(product, filt_ref[...], rows_ref)
@@ -121,55 +132,47 @@
         out_ref[:, 16 * pair : 16 * pair + 16, :] = jnp.concatenate(done, axis=1).astype(bf16)
 
 
-def gate_kernel(
-    feat_hbm, taps_hbm, spectra_hbm, gain_ref, queries_ref, direct_ref, feat_ref, taps_ref, ends_ref, rows_ref, sems
-):
+def gate_kernel(feat_hbm, taps_ref, spectra_ref, gain_ref, queries_ref, direct_ref, feat_ref, rows_ref, sem):
+    copy = pltpu.make_async_copy(feat_hbm, feat_ref, sem)
+    copy.start()
     device = lax.axis_index("seq")
-    ends = spectra_hbm.at[jnp.maximum(device - 1, 0), pl.ds(64, 16), :]
-    copies = [
-        pltpu.make_async_copy(s, d, sems.at[n])
-        for n, (s, d) in enumerate(((feat_hbm, feat_ref), (taps_hbm, taps_ref), (ends, ends_ref)))
-    ]
-    for copy in copies:
-        copy.start()
-    for copy in copies:
-        copy.wait()
-    edges = jnp.where(device > 0, ends_ref[...].astype(f32), 0.0)
-    mixed = [
-        short_filter(feat_ref[i].astype(f32), taps_ref[i], edges[4 * i : 4 * i + 4]) for i in range(3)
-    ]
+    ends = spectra_ref[jnp.maximum(device - 1, 0), 64:72, :].astype(f32)
+    ends = jnp.where(device > 0, ends, 0.0)
+    edges = [pltpu.roll(ends, 2, 1)[:4], ends[:4], ends[4:]]
+    copy.wait()
+    mixed = [short_filter(feat_ref[i].astype(f32), taps_ref[i], edges[i]) for i in range(3)]
     rows = to_blocks(mixed[0], mixed[1] * mixed[2], rows_ref)
     for c in range(4):
         queries_ref[c] = rows[c]
         direct_ref[c] = gain_ref[c] * rows[4 + c]
 
 
-def edge_terms(in_ref, taps_ref):
-    lane = lane_index((16, N2))
-    ends = [in_ref[block, 64:80, :].astype(f32) for block in range(SLICES)]
-    taps = jnp.concatenate([taps_ref[0], taps_ref[1], taps_ref[2], taps_ref[2]], axis=0)
-    taps = [jnp.broadcast_to(taps[:, k : k + 1], (16, N2)) for k in range(3)]
-
-    def products(tokens):
-        mixed = taps[2] * tokens + taps[1] * pltpu.roll(tokens, N2 - 1, 1) + taps[0] * pltpu.roll(tokens, N2 - 2, 1)
-        return mixed * pltpu.roll(mixed, 12, 0)
-
-    missing = [None]
-    for block in range(1, SLICES):
-        own = pltpu.roll(ends[block], 2, 1)
-        whole = jnp.where(lane < 2, pltpu.roll(ends[block - 1], 2, 1), own)
-        missing.append(products(whole) - products(jnp.where(lane < 2, 0.0, own)))
+def edge_terms(in_ref):
+    missing, given = [None], None
+    for block in range(SLICES):
+        ends = in_ref[block, 64:72, :].astype(f32)
+        own = ends + pltpu.roll(ends, N1, 1)
+        if block:
+            missing.append(own * pltpu.roll(given, 4, 0) + given * pltpu.roll(own + given, 4, 0))
+        given = pltpu.roll(own, N2 - 2, 1)
     return missing
 
 
-def mix_kernel(in_ref, taps_ref, wave_ref, out_ref):
+def wave_at(device):
+    row = lax.broadcasted_iota(jnp.int32, (8, N2), 0)
+    k = 4 * device + row % 4 + N1 * lane_index((8, N2))
+    angle = (k.astype(f32) + 0.25) * (-2.0 * math.pi / BLOCK)
+    return jnp.where(row < 4, jnp.cos(angle), jnp.sin(angle))
+
+
+def mix_kernel(in_ref, out_ref):
     top = lax.broadcasted_iota(jnp.int32, (8, N2), 0) < 4
-    missing = edge_terms(in_ref, taps_ref)
-    wave = wave_ref[lax.axis_index("seq")]
+    missing = edge_terms(in_ref)
+    wave = wave_at(lax.axis_index("seq"))
     for pair in range(2):
         sums = []
         for side in range(2):
-            row = 4 + 2 * pair + side
+            row = 2 * pair + side
             data, filt = [], []
             for block in range(SLICES):
                 both = in_ref[block, 16 * pair : 16 * pair + 16, :].astype(f32)
@@ -220,22 +223,14 @@
             out_ref[copy, N1 * c : N1 * (c + 1), :] = gated
 
 
-def wave_table():
-    row = np.arange(2 * N1)
-    k1 = 4 * (row // 8) + row % 4
-    angle = 2 * math.pi * (k1[:, None] + 64 * np.arange(N2)[None, :] + 0.25) / BLOCK
-    imag = (row // 4) % 2 == 1
-    return np.where(imag[:, None], -np.sin(angle), np.cos(angle)).astype(np.float32).reshape(SLICES, 8, N2)
-
-
 vmem = pl.BlockSpec(memory_space=pltpu.VMEM)
 smem = pl.BlockSpec(memory_space=pltpu.SMEM)
-anywhere = pl.BlockSpec(memory_space=pl.ANY)
-
-
-def call(kernel, specs, shape, dtype, *operands, scratch=()):
+hbm = pl.BlockSpec(memory_space=pltpu.HBM)
+
+
+def call(kernel, specs, shape, dtype, *operands, scratch=(), grant=32 << 20):
     if isinstance(shape, list):
-        out_shape, out_specs = [jax.ShapeDtypeStruct(s, dtype) for s in shape], [vmem] * len(shape)
+        out_shape, out_specs = [jax.ShapeDtypeStruct(s, d) for s, d in zip(shape, dtype)], [vmem] * len(shape)
     else:
         out_shape, out_specs = jax.ShapeDtypeStruct(shape, dtype), vmem
     return pl.pallas_call(
@@ -244,7 +239,7 @@
         in_specs=specs,
         out_specs=out_specs,
         scratch_shapes=scratch,
-        compiler_params=pltpu.CompilerParams(vmem_limit_bytes=32 << 20),
+        compiler_params=pltpu.CompilerParams(vmem_limit_bytes=grant),
         cost_estimate=pl.CostEstimate(flops=1 << 24, bytes_accessed=1 << 20, transcendentals=0),
     )(*operands)
 
@@ -255,33 +250,32 @@
     rows = pltpu.VMEM((8 * N1, N2), f32)
     spectra = call(
         forward_kernel,
-        [anywhere] * 7,
-        (SLICES, 80, N2),
+        [hbm] * 7,
+        (SLICES, 72, N2),
         bf16,
-        *held,
+        features,
+        short_taps,
+        *held[2:],
         scratch=[pltpu.VMEM(x.shape, x.dtype) for x in held] + [rows, pltpu.SemaphoreType.DMA((7,))],
+        grant=60 << 20,
     )
     spectra = lax.all_to_all(spectra, "seq", 0, 0, tiled=True)
     queries, direct = call(
         gate_kernel,
-        [anywhere] * 3 + [smem],
+        [hbm, vmem, vmem, smem],
         [(4, N1, N2)] * 2,
-        f32,
+        [f32] * 2,
         features,
         short_taps,
         spectra,
         skip_gain,
         scratch=[
             pltpu.VMEM(features.shape, bf16),
-            pltpu.VMEM(short_taps.shape, f32),
-            pltpu.VMEM((16, N2), bf16),
             rows,
-            pltpu.SemaphoreType.DMA((3,)),
+            pltpu.SemaphoreType.DMA(()),
         ],
     )
-    mixed = call(
-        mix_kernel, [vmem] * 3, (SLICES, 32, N2), bf16, spectra, short_taps, jnp.asarray(wave_table())
-    )
+    mixed = call(mix_kernel, [vmem], (SLICES, 32, N2), bf16, spectra)
     mixed = lax.all_to_all(mixed, "seq", 0, 0, tiled=True)
     return call(
         inverse_kernel,

time: 97 us -> 89.6 us (0.924)
  local copies, waits for them, and re-layouts: 7.84 us -> 1.03 us
  blocking collectives: 50.5 us -> 48.9 us
    unnamed x32 -> x16, local copies, waits for them, and re-layouts: 6.85 us -> 0.04 us
    all_to_all x1, blocking collectives: 30.8 us -> 29.5 us  [gated_copies(): spectra = lax.all_to_all(spectra, 'seq', 0, 0, tiled=True)]
  transfers between devices with their start and end apart: 2 -> 2, of which waited for: 2 -> 2; matrix products, arithmetic and copies ran while one was open for 1% -> 1% of each run, Pallas kernels for 1% -> 2%
where the time goes in v3:
time: 89.6 us; the launch traced here: 89.2 us
  blocking collectives  48.9 us (55%)
  starting transfers between devices  18.8 us (21%)
  waiting for transfers between devices  12.2 us (14%)
  Pallas kernels  6.03 us (7%)
  matrix products  2.07 us (2%)
  local copies, waits for them, and re-layouts  1.03 us (1%)
    all_to_all x1, blocking collectives, gated_copies(): spectra = lax.all_to_all(spectra, 'seq', 0, 0, tiled=True)  29.5 us
    all_to_all x1, blocking collectives, shards(): lax.all_to_all(sent, 'chan', 0, 0, tiled=True, axis_index_groups=same_core)  19.3 us
    all_to_all x1, starting transfers between devices, gated_copies(): mixed = lax.all_to_all(mixed, 'seq', 0, 0, tiled=True)  11.7 us
    all_to_all x1, waiting for transfers between devices, gated_copies(): mixed = lax.all_to_all(mixed, 'seq', 0, 0, tiled=True)  10.5 us
    ppermute x1, starting transfers between devices, shards(): other = lax.ppermute(own, 'chan', [(d, d ^ 1) for d in range(chan)])  7.16 us
    pallas_call x4, Pallas kernels, call(): pl.pallas_call(kernel, out_shape=out_shape, in_specs=specs, out_specs=out...  6.03 us
    dot_general x1, matrix products, shards(): lax.dot_general(rows, weight, (((0,), (0,)), ((), ())), preferred_element...  2.07 us
  transfers between devices with their start and end apart: 2, of which 2 were waited for; matrix products, arithmetic and copies ran while one was open for 1% of the time, Pallas kernels for 2%

profile of v3, /device:TPU:1, one launch (start us, length us, event | category | flops | bytes accessed | tf_op | source)
XLA Modules:
  0.0 89.2 jit_solution(4465260169148493833)
XLA Ops:
  0.0 0.0 copy-start.1
  0.0 0.0 copy-start.2
  0.0 0.0 copy-start.3
  0.0 0.0 copy-start.4
  0.0 0.0 copy-start.5
  0.0 0.0 copy-start
  0.0 0.0 copy-start.6
  0.1 2.8 %shard_map.109 = bf16[16,72,128]{2,1,0:T(8,128)(2,1)} custom-call(bf16[3,4,8192]{2,1,0:T(4,128)(2,1)} %feat_hbm.3, f32[3,4,3]{2,1,0:T(4,128)} %taps_ref.1, f32[4,8192]{1,0:T(4,128)} %filt_hbm.1, bf16[128,192]{1,0:T(8,128)(2,1)} %constant.38.clone.outer_hbm, f32[128,128]{1,0:T(8,128)} %constant.40.clone.cos_hbm.cos_ref, ...), custom_call_target="tpu_custom_call" | custom-call | flops 16777216 | bytes 1048576 | tf_op jit(solution)/shard_map/pallas_call | solution.py:236
  2.8 29.5 %all_to_all.15.in_ref.spectra_ref = bf16[16,72,128]{2,1,0:T(8,128)(2,1)S(1)} all-to-all(bf16[16,72,128]{2,1,0:T(8,128)(2,1)} %shard_map.109), channel_id=1, replica_groups=mesh['seq'=16,'chan'=32] {'seq'}, dimensions={0} | all-to-all | bytes 589824 | tf_op jit(solution)/shard_map/all_to_all | solution.py:262
  32.3 1.3 %shard_map.110 = bf16[16,32,128]{2,1,0:T(8,128)(2,1)} custom-call(bf16[16,72,128]{2,1,0:T(8,128)(2,1)S(1)} %all_to_all.15.in_ref.spectra_ref), custom_call_target="tpu_custom_call" | custom-call | flops 16777216 | bytes 1048576 | tf_op jit(solution)/shard_map/pallas_call | solution.py:236
  33.7 11.7 %all-to-all-start.1 = ((bf16[16,32,128]{2,1,0:T(8,128)(2,1)}), bf16[16,32,128]{2,1,0:T(8,128)(2,1)S(1)}, u32[]{:S(2)}, u32[]{:S(2)}) async-start(bf16[16,32,128]{2,1,0:T(8,128)(2,1)} %shard_map.110), calls=%async_computation.1 | async-start | bytes 262144 | tf_op jit(solution)/shard_map/all_to_all | solution.py:279
  45.4 0.0 copy-done.5
  45.4 0.0 copy-done
  45.4 0.0 copy-done.6
  45.4 1.4 %shard_map.111 = (f32[4,64,128]{2,1,0:T(8,128)S(1)}, f32[4,64,128]{2,1,0:T(8,128)S(1)}) custom-call(bf16[3,4,8192]{2,1,0:T(4,128)(2,1)S(1)} %copy-done, f32[3,4,3]{2,1,0:T(4,128)S(1)} %copy-done.5, bf16[16,72,128]{2,1,0:T(8,128)(2,1)S(1)} %all_to_all.15.in_ref.spectra_ref, f32[4]{0:T(128)S(1)} %copy-done.6), custom_call_target="tpu_custom_call" | custom-call | flops 16777216 | bytes 1048576 | tf_op jit(solution)/shard_map/pallas_call | solution.py:236
  46.8 0.0 copy-start.7
  46.8 10.5 %all-to-all-done.1.in_ref = bf16[16,32,128]{2,1,0:T(8,128)(2,1)S(1)} async-done(((bf16[16,32,128]{2,1,0:T(8,128)(2,1)}), bf16[16,32,128]{2,1,0:T(8,128)(2,1)S(1)}, u32[]{:S(2)}, u32[]{:S(2)}) %all-to-all-start.1) | async-done | bytes 131104 | tf_op jit(solution)/shard_map/all_to_all | solution.py:279
  57.4 0.0 copy-done.1
  57.4 0.0 copy-done.2
  57.4 0.0 copy-done.3
  57.4 0.0 copy-done.4
  57.4 0.5 shard_map.112
  57.9 19.3 %all_to_all.16 = bf16[16,256,128]{2,1,0:T(8,128)(2,1)S(1)} all-to-all(bf16[16,256,128]{2,1,0:T(8,128)(2,1)S(1)} %shard_map.112), channel_id=1, replica_groups={{0,2,4,6,8,10,12,14,16,18,20,22,24,26,28,30},{1,3,5,7,9,11,13,15,17,19,..., dimensions={0} | all-to-all | bytes 2097152 | tf_op jit(solution)/shard_map/all_to_all | solution.py:300
  77.3 7.2 %collective-permute-start = (bf16[16,256,128]{2,1,0:T(8,128)(2,1)S(1)}, bf16[16,256,128]{2,1,0:T(8,128)(2,1)S(1)}, u32[]{:S(2)}, u32[]{:S(2)}) collective-permute-start(bf16[16,256,128]{2,1,0:T(8,128)(2,1)S(1)} %all_to_all.16), channel_id=1, source_target_pairs={{0,1},{1,0},{2,3},{3,2},{4,5},{5,4},{6,7},{7,6},{8,9},{9,8},{10,11... | collective-permute-start | bytes 3145736 | tf_op jit(solution)/shard_map/ppermute | solution.py:301
  84.4 0.0 copy-done.7
  84.5 0.5 reshape.17
  85.0 1.7 %collective-permute-done = bf16[16,256,128]{2,1,0:T(8,128)(2,1)S(1)} collective-permute-done((bf16[16,256,128]{2,1,0:T(8,128)(2,1)S(1)}, bf16[16,256,128]{2,1,0:T(8,128)(2,1)S(1)}, u32[]{:S(2)}, u32[]{:S(2)}) %collective-permute-start) | collective-permute-done | bytes 1048608 | tf_op jit(solution)/shard_map/ppermute | solution.py:301
  86.7 0.5 reshape.18
  87.2 2.1 %convolution_convert_fusion = bf16[8192,128]{1,0:T(8,128)(2,1)} fusion(bf16[64,8192]{1,0:T(8,128)(2,1)S(1)} %reshape.18, bf16[64,8192]{1,0:T(8,128)(2,1)S(1)} %reshape.17, bf16[64,128]{1,0:T(8,128)(2,1)S(1)} %bitcast.4, bf16[64,128]{1,0:T(8,128)(2,1)S(1)} %bitcast.3), kind=kOutput, calls=%fused_computation | convolution fusion | flops 273743872 | bytes 4227072 | tf_op jit(solution)/shard_map/dot_general | solution.py:308
  (1 shorter events, 0.0 us)
Async XLA Ops:
  0.0 57.4 %copy-start.1 = (f32[128,128]{1,0:T(8,128)S(1)}, f32[128,128]{1,0:T(8,128)}, u32[]{:S(2)}) copy-start(f32[128,128]{1,0:T(8,128)} %constant.41.clone.sin_hbm.sin_ref) | copy-start | bytes 196612
  0.0 57.4 %copy-start.2 = (f32[128,128]{1,0:T(8,128)S(1)}, f32[128,128]{1,0:T(8,128)}, u32[]{:S(2)}) copy-start(f32[128,128]{1,0:T(8,128)} %constant.40.clone.cos_hbm.cos_ref) | copy-start | bytes 196612
  0.0 57.4 %copy-start.3 = (bf16[384,256]{1,0:T(8,128)(2,1)S(1)}, bf16[384,256]{1,0:T(8,128)(2,1)}, u32[]{:S(2)}) copy-start(bf16[384,256]{1,0:T(8,128)(2,1)} %constant.43.clone.inner_ref) | copy-start | bytes 589828
  0.0 57.4 %copy-start.4 = (bf16[64,384]{1,0:T(8,128)(2,1)S(1)}, bf16[64,384]{1,0:T(8,128)(2,1)}, u32[]{:S(2)}) copy-start(bf16[64,384]{1,0:T(8,128)(2,1)} %constant.39.clone.outer_ref) | copy-start | bytes 147460
  0.0 45.3 %copy-start.5 = (f32[3,4,3]{2,1,0:T(4,128)S(1)}, f32[3,4,3]{2,1,0:T(4,128)}, u32[]{:S(2)}) copy-start(f32[3,4,3]{2,1,0:T(4,128)} %taps_ref.1) | copy-start | bytes 436
  0.0 45.3 %copy-start = (bf16[3,4,8192]{2,1,0:T(4,128)(2,1)S(1)}, bf16[3,4,8192]{2,1,0:T(4,128)(2,1)}, u32[]{:S(2)}) copy-start(bf16[3,4,8192]{2,1,0:T(4,128)(2,1)} %feat_hbm.3) | copy-start | bytes 589828
  0.0 45.3 %copy-start.6 = (f32[4]{0:T(128)S(1)}, f32[4]{0:T(128)}, u32[]{:S(2)}) copy-start(f32[4]{0:T(128)} %gain_ref.1) | copy-start | bytes 52
  33.7 23.7 %all-to-all-start.1 = ((bf16[16,32,128]{2,1,0:T(8,128)(2,1)}), bf16[16,32,128]{2,1,0:T(8,128)(2,1)S(1)}, u32[]{:S(2)}, u32[]{:S(2)}) async-start(bf16[16,32,128]{2,1,0:T(8,128)(2,1)} %shard_map.110), calls=%async_computation.1 | async-start | bytes 262144 | tf_op jit(solution)/shard_map/all_to_all | solution.py:279
  46.8 37.6 %copy-start.7 = (bf16[128,128]{1,0:T(8,128)(2,1)S(1)}, bf16[128,128]{1,0:T(8,128)(2,1)}, u32[]{:S(2)}) copy-start(bf16[128,128]{1,0:T(8,128)(2,1)} %param.15) | copy-start | bytes 98308
  77.3 9.4 %collective-permute-start = (bf16[16,256,128]{2,1,0:T(8,128)(2,1)S(1)}, bf16[16,256,128]{2,1,0:T(8,128)(2,1)S(1)}, u32[]{:S(2)}, u32[]{:S(2)}) collective-permute-start(bf16[16,256,128]{2,1,0:T(8,128)(2,1)S(1)} %all_to_all.16), channel_id=1, source_target_pairs={{0,1},{1,0},{2,3},{3,2},{4,5},{5,4},{6,7},{7,6},{8,9},{9,8},{10,11... | collective-permute-start | bytes 3145736 | tf_op jit(solution)/shard_map/ppermute | solution.py:301

commit v4 on v3

--- a/solution.py
+++ b/solution.py
@@ -12,6 +12,8 @@
 N1, N2 = 64, 128
 BLOCK = N1 * N2
 SLICES = 16
+OUT, BACK = 10, 8
+FIRST_CHIP = 14
 f32, bf16 = jnp.float32, jnp.bfloat16
 
 
@@ -136,7 +138,7 @@
     copy = pltpu.make_async_copy(feat_hbm, feat_ref, sem)
     copy.start()
     device = lax.axis_index("seq")
-    ends = spectra_ref[jnp.maximum(device - 1, 0), 64:72, :].astype(f32)
+    ends = spectra_ref[(device + SLICES - 1 - OUT) % SLICES, 64:72, :].astype(f32)
     ends = jnp.where(device > 0, ends, 0.0)
     edges = [pltpu.roll(ends, 2, 1)[:4], ends[:4], ends[4:]]
     copy.wait()
@@ -147,10 +149,19 @@
         direct_ref[c] = gain_ref[c] * rows[4 + c]
 
 
+def slot(block, first):
+    return (block - first) % SLICES
+
+
+def over_seq(value, first):
+    group = [(j + first) % SLICES for j in range(SLICES)]
+    return lax.all_to_all(value, "seq", 0, 0, tiled=True, axis_index_groups=[group])
+
+
 def edge_terms(in_ref):
     missing, given = [None], None
     for block in range(SLICES):
-        ends = in_ref[block, 64:72, :].astype(f32)
+        ends = in_ref[slot(block, OUT), 64:72, :].astype(f32)
         own = ends + pltpu.roll(ends, N1, 1)
         if block:
             missing.append(own * pltpu.roll(given, 4, 0) + given * pltpu.roll(own + given, 4, 0))
@@ -168,20 +179,20 @@
 def mix_kernel(in_ref, out_ref):
     top = lax.broadcasted_iota(jnp.int32, (8, N2), 0) < 4
     missing = edge_terms(in_ref)
-    wave = wave_at(lax.axis_index("seq"))
+    wave = wave_at((lax.axis_index("seq") + SLICES - OUT) % SLICES)
     for pair in range(2):
         sums = []
         for side in range(2):
             row = 2 * pair + side
             data, filt = [], []
             for block in range(SLICES):
-                both = in_ref[block, 16 * pair : 16 * pair + 16, :].astype(f32)
+                both = in_ref[slot(block, OUT), 16 * pair : 16 * pair + 16, :].astype(f32)
                 tile = both[8 * side : 8 * side + 8]
                 if block:
                     lack = missing[block][row : row + 1]
                     tile = tile + jnp.where(top, lack[:, 0:1], 0.0) + lack[:, 1:2] * wave
                 data.append(tile)
-                both = in_ref[block, 32 + 16 * pair : 48 + 16 * pair, :].astype(f32)
+                both = in_ref[slot(block, OUT), 32 + 16 * pair : 48 + 16 * pair, :].astype(f32)
                 filt.append(both[8 * side : 8 * side + 8])
             swapped = [pltpu.roll(tile, 4, 0) for tile in data]
             real_parts, imag_parts = [], []
@@ -202,15 +213,15 @@
                 row.append(total)
             sums.append(row)
         for d in range(SLICES):
-            out_ref[d, 16 * pair : 16 * pair + 16, :] = jnp.concatenate([sums[0][d], sums[1][d]], axis=0).astype(bf16)
+            out_ref[slot(d, BACK), 16 * pair : 16 * pair + 16, :] = jnp.concatenate([sums[0][d], sums[1][d]], axis=0).astype(bf16)
 
 
 def inverse_kernel(in_ref, queries_ref, direct_ref, outer_ref, cos_ref, sin_ref, inner_ref, out_ref):
     turned = []
     for pair in range(2):
-        both = in_ref[:, 16 * pair : 16 * pair + 16, :].astype(f32)
+        both = [in_ref[slot(p + OUT, BACK), 16 * pair : 16 * pair + 16, :].astype(f32) for p in range(SLICES)]
         for side in range(2):
-            tile = both[:, 8 * side : 8 * side + 8, :].reshape(2 * N1, N2)
+            tile = jnp.concatenate([part[8 * side : 8 * side + 8] for part in both], axis=0)
             tile = inner_stage(tile, inner_ref[...])
             turned.append(tile * cos_ref[...] - halves_swapped(tile) * sin_ref[...])
     high, low = split(jnp.concatenate(turned, axis=1))
@@ -259,7 +270,7 @@
         scratch=[pltpu.VMEM(x.shape, x.dtype) for x in held] + [rows, pltpu.SemaphoreType.DMA((7,))],
         grant=60 << 20,
     )
-    spectra = lax.all_to_all(spectra, "seq", 0, 0, tiled=True)
+    spectra = over_seq(spectra, OUT)
     queries, direct = call(
         gate_kernel,
         [hbm, vmem, vmem, smem],
@@ -276,7 +287,7 @@
         ],
     )
     mixed = call(mix_kernel, [vmem], (SLICES, 32, N2), bf16, spectra)
-    mixed = lax.all_to_all(mixed, "seq", 0, 0, tiled=True)
+    mixed = over_seq(mixed, BACK)
     return call(
         inverse_kernel,
         [vmem] * 7,
@@ -292,19 +303,22 @@
     )
 
 
+def gather_groups(chips):
+    order = [(chip + FIRST_CHIP) % chips for chip in range(chips)]
+    return [[2 * chip + core for chip in order] for core in range(2)]
+
+
 def shards(features, short_taps, long_filter, skip_gain, out_weight):
     chan = lax.axis_size("chan")
     chips = chan // 2
+    groups = gather_groups(chips)
     sent = gated_copies(features, short_taps, long_filter, skip_gain, chips)
-    same_core = [[2 * chip + core for chip in range(chips)] for core in range(2)]
-    own = lax.all_to_all(sent, "chan", 0, 0, tiled=True, axis_index_groups=same_core)
+    own = lax.all_to_all(sent, "chan", 0, 0, tiled=True, axis_index_groups=groups)
     other = lax.ppermute(own, "chan", [(d, d ^ 1) for d in range(chan)])
-    core = lax.axis_index("chan") % 2
-    weight = out_weight.reshape(chips, 2, 4, N2)
-    own_weight = lax.dynamic_index_in_dim(weight, core, 1, False).reshape(4 * chips, N2)
-    other_weight = lax.dynamic_index_in_dim(weight, 1 - core, 1, False).reshape(4 * chips, N2)
+    blocks = out_weight.reshape(chan, 4, N2)
+    sides = [jnp.concatenate([blocks[d] for d in groups[g] + groups[1 - g]], axis=0) for g in range(2)]
+    weight = jnp.where(lax.axis_index("chan") % 2 == 0, sides[0], sides[1])
     rows = jnp.concatenate([own.reshape(4 * chips, BLOCK), other.reshape(4 * chips, BLOCK)], axis=0)
-    weight = jnp.concatenate([own_weight, other_weight], axis=0)
     projected = lax.dot_general(rows, weight, (((0,), (0,)), ((), ())), preferred_element_type=f32)
     return projected.astype(bf16)
 

time: 89.6 us -> 82.8 us (0.924)
  waiting for transfers between devices: 12.2 us -> 4.96 us
  starting transfers between devices: 18.8 us -> 17.5 us
  local copies, waits for them, and re-layouts: 1.03 us -> 1.96 us
  blocking collectives: 48.9 us -> 49.8 us
    all_to_all x1, waiting for transfers between devices: 10.5 us -> 4.2 us  [over_seq(): lax.all_to_all(value, 'seq', 0, 0, tiled=True, axis_index_groups=[group])]
    ppermute x1, starting transfers between devices: 7.16 us -> 5.35 us  [shards(): other = lax.ppermute(own, 'chan', [(d, d ^ 1) for d in range(chan)])]
    ppermute x1, waiting for transfers between devices: 1.71 us -> 0.76 us  [shards(): other = lax.ppermute(own, 'chan', [(d, d ^ 1) for d in range(chan)])]
    all_to_all x2, blocking collectives: 48.9 us -> 49.8 us  [the longest x1 31.5 us: over_seq(): lax.all_to_all(value, 'seq', 0, 0, tiled=True, axis_index_groups=[group])]
    concatenate x0 -> x2, local copies, waits for them, and re-layouts: none -> 0.94 us  [shards(): jnp.concatenate([blocks[d] for d in groups[g] + groups[1 - g]], axis=0)]
  transfers between devices with their start and end apart: 2 -> 2, of which waited for: 2 -> 2; matrix products, arithmetic and copies ran while one was open for 1% -> 2% of each run, Pallas kernels for 2% -> 2%
where the time goes in v4:
time: 82.8 us; the launch traced here: 82.5 us
  blocking collectives  49.8 us (60%)
  starting transfers between devices  17.5 us (21%)
  Pallas kernels  6.03 us (7%)
  waiting for transfers between devices  4.96 us (6%)
  matrix products  2.08 us (3%)
  local copies, waits for them, and re-layouts  1.96 us (2%)
    all_to_all x1, blocking collectives, over_seq(): lax.all_to_all(value, 'seq', 0, 0, tiled=True, axis_index_groups=[group])  31.5 us
    all_to_all x1, blocking collectives, shards(): lax.all_to_all(sent, 'chan', 0, 0, tiled=True, axis_index_groups=groups)  18.3 us
    all_to_all x1, starting transfers between devices, over_seq(): lax.all_to_all(value, 'seq', 0, 0, tiled=True, axis_index_groups=[group])  12.2 us
    pallas_call x4, Pallas kernels, call(): pl.pallas_call(kernel, out_shape=out_shape, in_specs=specs, out_specs=out...  6.03 us
    ppermute x1, starting transfers between devices, shards(): other = lax.ppermute(own, 'chan', [(d, d ^ 1) for d in range(chan)])  5.35 us
    all_to_all x1, waiting for transfers between devices, over_seq(): lax.all_to_all(value, 'seq', 0, 0, tiled=True, axis_index_groups=[group])  4.2 us
    dot_general x1, matrix products, shards(): lax.dot_general(rows, weight, (((0,), (0,)), ((), ())), preferred_element...  2.08 us
  transfers between devices with their start and end apart: 2, of which 2 were waited for; matrix products, arithmetic and copies ran while one was open for 2% of the time, Pallas kernels for 2%

profile of v4, /device:TPU:1, one launch (start us, length us, event | category | flops | bytes accessed | tf_op | source)
XLA Modules:
  0.0 82.5 jit_solution(5484051896681125612)
XLA Ops:
  0.0 0.0 copy-start.1
  0.0 0.0 copy-start.2
  0.0 0.0 copy-start.3
  0.0 0.0 copy-start.4
  0.0 0.0 copy-start.5
  0.0 0.0 copy-start
  0.0 0.0 copy-start.6
  0.1 2.8 %shard_map.109 = bf16[16,72,128]{2,1,0:T(8,128)(2,1)} custom-call(bf16[3,4,8192]{2,1,0:T(4,128)(2,1)} %feat_hbm.3, f32[3,4,3]{2,1,0:T(4,128)} %taps_ref.1, f32[4,8192]{1,0:T(4,128)} %filt_hbm.1, bf16[128,192]{1,0:T(8,128)(2,1)} %constant.30.clone.outer_hbm, f32[128,128]{1,0:T(8,128)} %constant.32.clone.cos_hbm.cos_ref, ...), custom_call_target="tpu_custom_call" | custom-call | flops 16777216 | bytes 1048576 | tf_op jit(solution)/shard_map/pallas_call | solution.py:247
  2.8 31.5 %all_to_all.15.in_ref.spectra_ref = bf16[16,72,128]{2,1,0:T(8,128)(2,1)S(1)} all-to-all(bf16[16,72,128]{2,1,0:T(8,128)(2,1)} %shard_map.109), channel_id=1, replica_groups={{320,352,384,416,448,480,0,32,64,96,128,160,192,224,256,288},{321,353,3..., dimensions={0} | all-to-all | bytes 589824 | tf_op jit(solution)/shard_map/all_to_all | solution.py:158
  34.3 1.3 %shard_map.110 = bf16[16,32,128]{2,1,0:T(8,128)(2,1)} custom-call(bf16[16,72,128]{2,1,0:T(8,128)(2,1)S(1)} %all_to_all.15.in_ref.spectra_ref), custom_call_target="tpu_custom_call" | custom-call | flops 16777216 | bytes 1048576 | tf_op jit(solution)/shard_map/pallas_call | solution.py:247
  35.7 12.2 %all-to-all-start.1 = ((bf16[16,32,128]{2,1,0:T(8,128)(2,1)}), bf16[16,32,128]{2,1,0:T(8,128)(2,1)S(1)}, u32[]{:S(2)}, u32[]{:S(2)}) async-start(bf16[16,32,128]{2,1,0:T(8,128)(2,1)} %shard_map.110), calls=%async_computation.1 | async-start | bytes 262144 | tf_op jit(solution)/shard_map/all_to_all | solution.py:158
  47.8 0.0 copy-done.5
  47.8 0.0 copy-done
  47.8 0.0 copy-done.6
  47.9 1.4 %shard_map.111 = (f32[4,64,128]{2,1,0:T(8,128)S(1)}, f32[4,64,128]{2,1,0:T(8,128)S(1)}) custom-call(bf16[3,4,8192]{2,1,0:T(4,128)(2,1)S(1)} %copy-done, f32[3,4,3]{2,1,0:T(4,128)S(1)} %copy-done.5, bf16[16,72,128]{2,1,0:T(8,128)(2,1)S(1)} %all_to_all.15.in_ref.spectra_ref, f32[4]{0:T(128)S(1)} %copy-done.6), custom_call_target="tpu_custom_call" | custom-call | flops 16777216 | bytes 1048576 | tf_op jit(solution)/shard_map/pallas_call | solution.py:247
  49.3 0.0 copy-start.7
  49.3 4.2 %all-to-all-done.1.in_ref = bf16[16,32,128]{2,1,0:T(8,128)(2,1)S(1)} async-done(((bf16[16,32,128]{2,1,0:T(8,128)(2,1)}), bf16[16,32,128]{2,1,0:T(8,128)(2,1)S(1)}, u32[]{:S(2)}, u32[]{:S(2)}) %all-to-all-start.1) | async-done | bytes 131104 | tf_op jit(solution)/shard_map/all_to_all | solution.py:158
  53.5 0.0 copy-done.1
  53.5 0.0 copy-done.2
  53.5 0.0 copy-done.3
  53.5 0.0 copy-done.4
  53.5 0.5 shard_map.112
  54.0 18.3 %all_to_all.16 = bf16[16,256,128]{2,1,0:T(8,128)(2,1)S(1)} all-to-all(bf16[16,256,128]{2,1,0:T(8,128)(2,1)S(1)} %shard_map.112), channel_id=1, replica_groups={{28,30,0,2,4,6,8,10,12,14,16,18,20,22,24,26},{29,31,1,3,5,7,9,11,13,15,..., dimensions={0} | all-to-all | bytes 2097152 | tf_op jit(solution)/shard_map/all_to_all | solution.py:316
  72.3 5.3 %collective-permute-start = (bf16[16,256,128]{2,1,0:T(8,128)(2,1)S(1)}, bf16[16,256,128]{2,1,0:T(8,128)(2,1)S(1)}, u32[]{:S(2)}, u32[]{:S(2)}) collective-permute-start(bf16[16,256,128]{2,1,0:T(8,128)(2,1)S(1)} %all_to_all.16), channel_id=1, source_target_pairs={{0,1},{1,0},{2,3},{3,2},{4,5},{5,4},{6,7},{7,6},{8,9},{9,8},{10,11... | collective-permute-start | bytes 3145736 | tf_op jit(solution)/shard_map/ppermute | solution.py:317
  77.7 0.0 copy-done.7
  77.8 0.5 concatenate.12
  78.3 0.4 concatenate.11
  78.7 0.5 reshape.71
  79.2 0.8 collective-permute-done
  79.9 0.5 reshape.72
  80.4 2.1 %convolution_convert_fusion = bf16[8192,128]{1,0:T(8,128)(2,1)} fusion(bf16[64,8192]{1,0:T(8,128)(2,1)S(1)} %reshape.72, bf16[64,8192]{1,0:T(8,128)(2,1)S(1)} %reshape.71, bf16[128,128]{1,0:T(8,128)(2,1)S(1)} %concatenate.11, bf16[128,128]{1,0:T(8,128)(2,1)S(1)} %concatenate.12, pred[]{:T(512)S(6)} %eq.5), kind=kOutput, calls=%fused_computation | convolution fusion | flops 273694720 | bytes 4259841 | tf_op jit(solution)/shard_map/dot_general | solution.py:322
  (3 shorter events, 0.0 us)
Async XLA Ops:
  0.0 53.5 %copy-start.1 = (f32[128,128]{1,0:T(8,128)S(1)}, f32[128,128]{1,0:T(8,128)}, u32[]{:S(2)}) copy-start(f32[128,128]{1,0:T(8,128)} %constant.33.clone.sin_hbm.sin_ref) | copy-start | bytes 196612
  0.0 53.5 %copy-start.2 = (f32[128,128]{1,0:T(8,128)S(1)}, f32[128,128]{1,0:T(8,128)}, u32[]{:S(2)}) copy-start(f32[128,128]{1,0:T(8,128)} %constant.32.clone.cos_hbm.cos_ref) | copy-start | bytes 196612
  0.0 53.5 %copy-start.3 = (bf16[384,256]{1,0:T(8,128)(2,1)S(1)}, bf16[384,256]{1,0:T(8,128)(2,1)}, u32[]{:S(2)}) copy-start(bf16[384,256]{1,0:T(8,128)(2,1)} %constant.35.clone.inner_ref) | copy-start | bytes 589828
  0.0 53.5 %copy-start.4 = (bf16[64,384]{1,0:T(8,128)(2,1)S(1)}, bf16[64,384]{1,0:T(8,128)(2,1)}, u32[]{:S(2)}) copy-start(bf16[64,384]{1,0:T(8,128)(2,1)} %constant.31.clone.outer_ref) | copy-start | bytes 147460
  0.0 47.8 %copy-start.5 = (f32[3,4,3]{2,1,0:T(4,128)S(1)}, f32[3,4,3]{2,1,0:T(4,128)}, u32[]{:S(2)}) copy-start(f32[3,4,3]{2,1,0:T(4,128)} %taps_ref.1) | copy-start | bytes 436
  0.0 47.8 %copy-start = (bf16[3,4,8192]{2,1,0:T(4,128)(2,1)S(1)}, bf16[3,4,8192]{2,1,0:T(4,128)(2,1)}, u32[]{:S(2)}) copy-start(bf16[3,4,8192]{2,1,0:T(4,128)(2,1)} %feat_hbm.3) | copy-start | bytes 589828
  0.0 47.8 %copy-start.6 = (f32[4]{0:T(128)S(1)}, f32[4]{0:T(128)}, u32[]{:S(2)}) copy-start(f32[4]{0:T(128)} %gain_ref.1) | copy-start | bytes 52
  35.7 17.8 %all-to-all-start.1 = ((bf16[16,32,128]{2,1,0:T(8,128)(2,1)}), bf16[16,32,128]{2,1,0:T(8,128)(2,1)S(1)}, u32[]{:S(2)}, u32[]{:S(2)}) async-start(bf16[16,32,128]{2,1,0:T(8,128)(2,1)} %shard_map.110), calls=%async_computation.1 | async-start | bytes 262144 | tf_op jit(solution)/shard_map/all_to_all | solution.py:158
  49.3 28.4 %copy-start.7 = (bf16[128,128]{1,0:T(8,128)(2,1)S(1)}, bf16[128,128]{1,0:T(8,128)(2,1)}, u32[]{:S(2)}) copy-start(bf16[128,128]{1,0:T(8,128)(2,1)} %param.15) | copy-start | bytes 98308
  72.3 7.6 %collective-permute-start = (bf16[16,256,128]{2,1,0:T(8,128)(2,1)S(1)}, bf16[16,256,128]{2,1,0:T(8,128)(2,1)S(1)}, u32[]{:S(2)}, u32[]{:S(2)}) collective-permute-start(bf16[16,256,128]{2,1,0:T(8,128)(2,1)S(1)} %all_to_all.16), channel_id=1, source_target_pairs={{0,1},{1,0},{2,3},{3,2},{4,5},{5,4},{6,7},{7,6},{8,9},{9,8},{10,11... | collective-permute-start | bytes 3145736 | tf_op jit(solution)/shard_map/ppermute | solution.py:317

commit v5 on v4

--- a/solution.py
+++ b/solution.py
@@ -12,7 +12,7 @@
 N1, N2 = 64, 128
 BLOCK = N1 * N2
 SLICES = 16
-OUT, BACK = 10, 8
+OUT, BACK = 12, 8
 FIRST_CHIP = 14
 f32, bf16 = jnp.float32, jnp.bfloat16
 
@@ -88,11 +88,11 @@
     return [rows_ref[pl.ds(s, N1, stride=8), :] for s in range(8)]
 
 
-def block_ends(streams, taps_ref):
+def block_ends(query, streams, taps_ref):
     lane = lane_index((8, N2))
-    first = jnp.concatenate([stream[:, :N2] for stream in streams[1:]], axis=0)
-    last = jnp.concatenate([stream[:, BLOCK - N2 :] for stream in streams[1:]], axis=0)
-    query = jnp.concatenate([streams[0][:, BLOCK - N2 :]] * 2, axis=0)
+    first = jnp.concatenate([stream[:, :N2] for stream in streams], axis=0)
+    last = jnp.concatenate([stream[:, BLOCK - N2 :] for stream in streams], axis=0)
+    query = jnp.concatenate([query] * 2, axis=0)
     taps = jnp.concatenate([taps_ref[1], taps_ref[2]], axis=0)
     own = taps[:, 0:1] * first + jnp.where(lane == 1, taps[:, 1:2] * pltpu.roll(first, 1, 1), 0.0)
     given = taps[:, 2:3] * last + jnp.where(lane == N2 - 2, taps[:, 1:2] * pltpu.roll(last, N2 - 1, 1), 0.0)
@@ -104,25 +104,25 @@
 
 def forward_kernel(
     feat_hbm, taps_hbm, filt_hbm, outer_hbm, cos_hbm, sin_hbm, inner_hbm, out_ref,
-    feat_ref, taps_ref, filt_ref, outer_ref, cos_ref, sin_ref, inner_ref, rows_ref, sems,
+    feat_ref, taps_ref, filt_ref, outer_ref, cos_ref, sin_ref, inner_ref, last_ref, rows_ref, sems,
 ):
-    sources = (feat_hbm, taps_hbm, filt_hbm, outer_hbm, cos_hbm, sin_hbm, inner_hbm)
-    places = (feat_ref, taps_ref, filt_ref, outer_ref, cos_ref, sin_ref, inner_ref)
+    last = pl.ds(BLOCK - N2, N2)
+    sources = (feat_hbm.at[1:3], filt_hbm, taps_hbm, feat_hbm.at[0, :, last], outer_hbm, inner_hbm, cos_hbm, sin_hbm)
+    places = (feat_ref, filt_ref, taps_ref, last_ref, outer_ref, inner_ref, cos_ref, sin_ref)
     copies = [pltpu.make_async_copy(s, d, sems.at[n]) for n, (s, d) in enumerate(zip(sources, places))]
     for copy in copies:
         copy.start()
-    for copy in copies[:2]:
+    for copy in copies[:4]:
         copy.wait()
-    streams = [feat_ref[i].astype(f32) for i in range(3)]
-    ends = block_ends(streams, taps_ref).astype(bf16)
+    streams = [feat_ref[i].astype(f32) for i in range(2)]
+    ends = block_ends(last_ref[...].astype(f32), streams, taps_ref).astype(bf16)
     for device in range(SLICES):
         out_ref[device, 64:72, :] = ends
-    product = short_filter(streams[1], taps_ref[1]) * short_filter(streams[2], taps_ref[2])
-    copies[2].wait()
+    product = short_filter(streams[0], taps_ref[1]) * short_filter(streams[1], taps_ref[2])
     signals = to_blocks(product, filt_ref[...], rows_ref)
     high, low = split(jnp.concatenate(signals, axis=1))
     stacked = jnp.concatenate([high, low, high], axis=0)
-    for copy in copies[3:]:
+    for copy in copies[4:]:
         copy.wait()
     first = jnp.dot(outer_ref[...], stacked, preferred_element_type=f32)
     for pair in range(4):
@@ -258,17 +258,17 @@
 def gated_copies(features, short_taps, long_filter, skip_gain, copies):
     forward_outer, inverse_outer, turn_cos, turn_sin, forward_inner, inverse_inner = map(jnp.asarray, tables())
     held = (features, short_taps, long_filter, forward_outer, turn_cos, turn_sin, forward_inner)
+    held = [pltpu.with_memory_space_constraint(x, pltpu.HBM) for x in held]
     rows = pltpu.VMEM((8 * N1, N2), f32)
     spectra = call(
         forward_kernel,
         [hbm] * 7,
         (SLICES, 72, N2),
         bf16,
-        features,
-        short_taps,
-        *held[2:],
-        scratch=[pltpu.VMEM(x.shape, x.dtype) for x in held] + [rows, pltpu.SemaphoreType.DMA((7,))],
-        grant=60 << 20,
+        *held,
+        scratch=[pltpu.VMEM((2, 4, BLOCK), bf16)]
+        + [pltpu.VMEM(x.shape, x.dtype) for x in held[1:]]
+        + [pltpu.VMEM((4, N2), bf16), rows, pltpu.SemaphoreType.DMA((8,))],
     )
     spectra = over_seq(spectra, OUT)
     queries, direct = call(

time: 82.8 us -> 81.2 us (0.981)
  starting transfers between devices: 17.5 us -> 20.6 us
  blocking collectives: 49.8 us -> 47 us
  waiting for transfers between devices: 4.96 us -> 3.84 us
    all_to_all x1, blocking collectives: 18.3 us -> 16.7 us  [shards(): lax.all_to_all(sent, 'chan', 0, 0, tiled=True, axis_index_groups=groups)]
    all_to_all x1, starting transfers between devices: 12.2 us -> 13.7 us  [over_seq(): lax.all_to_all(value, 'seq', 0, 0, tiled=True, axis_index_groups=[group])]
    ppermute x1, starting transfers between devices: 5.35 us -> 6.87 us  [shards(): other = lax.ppermute(own, 'chan', [(d, d ^ 1) for d in range(chan)])]
    all_to_all x1, blocking collectives: 31.5 us -> 30.3 us  [over_seq(): lax.all_to_all(value, 'seq', 0, 0, tiled=True, axis_index_groups=[group])]
    all_to_all x1, waiting for transfers between devices: 4.2 us -> 3.08 us  [over_seq(): lax.all_to_all(value, 'seq', 0, 0, tiled=True, axis_index_groups=[group])]
where the time goes in v5:
time: 81.2 us; the launch traced here: 81 us
  blocking collectives  47 us (58%)
  starting transfers between devices  20.6 us (25%)
  Pallas kernels  5.35 us (7%)
  waiting for transfers between devices  3.84 us (5%)
  matrix products  2.07 us (3%)
  local copies, waits for them, and re-layouts  1.96 us (2%)
    all_to_all x1, blocking collectives, over_seq(): lax.all_to_all(value, 'seq', 0, 0, tiled=True, axis_index_groups=[group])  30.3 us
    all_to_all x1, blocking collectives, shards(): lax.all_to_all(sent, 'chan', 0, 0, tiled=True, axis_index_groups=groups)  16.7 us
    all_to_all x1, starting transfers between devices, over_seq(): lax.all_to_all(value, 'seq', 0, 0, tiled=True, axis_index_groups=[group])  13.7 us
    ppermute x1, starting transfers between devices, shards(): other = lax.ppermute(own, 'chan', [(d, d ^ 1) for d in range(chan)])  6.87 us
    pallas_call x4, Pallas kernels, call(): pl.pallas_call(kernel, out_shape=out_shape, in_specs=specs, out_specs=out...  5.35 us
    all_to_all x1, waiting for transfers between devices, over_seq(): lax.all_to_all(value, 'seq', 0, 0, tiled=True, axis_index_groups=[group])  3.08 us
    dot_general x1, matrix products, shards(): lax.dot_general(rows, weight, (((0,), (0,)), ((), ())), preferred_element...  2.07 us
  transfers between devices with their start and end apart: 2, of which 2 were waited for; matrix products, arithmetic and copies ran while one was open for 2% of the time, Pallas kernels for 2%

profile of v5, /device:TPU:1, one launch (start us, length us, event | category | flops | bytes accessed | tf_op | source)
XLA Modules:
  0.0 81.0 jit_solution(8401315403863960972)
XLA Ops:
  0.0 0.0 copy-start.1
  0.0 0.0 copy-start.2
  0.0 0.0 copy-start.3
  0.0 0.0 copy-start.4
  0.0 0.0 copy-start.5
  0.0 0.0 copy-start
  0.0 0.0 copy-start.6
  0.1 2.1 %shard_map.109 = bf16[16,72,128]{2,1,0:T(8,128)(2,1)S(1)} custom-call(bf16[3,4,8192]{2,1,0:T(4,128)(2,1)} %feat_hbm.3, f32[3,4,3]{2,1,0:T(4,128)} %taps_ref.1, f32[4,8192]{1,0:T(4,128)} %filt_hbm.1, bf16[128,192]{1,0:T(8,128)(2,1)} %constant.30.clone.outer_hbm, f32[128,128]{1,0:T(8,128)} %constant.32.clone.cos_hbm.cos_ref, ...), custom_call_target="tpu_custom_call" | custom-call | flops 16777216 | bytes 1048576 | tf_op jit(solution)/shard_map/pallas_call | solution.py:247
  2.2 30.3 %all_to_all.15.in_ref.spectra_ref = bf16[16,72,128]{2,1,0:T(8,128)(2,1)S(1)} all-to-all(bf16[16,72,128]{2,1,0:T(8,128)(2,1)S(1)} %shard_map.109), channel_id=1, replica_groups={{384,416,448,480,0,32,64,96,128,160,192,224,256,288,320,352},{385,417,4..., dimensions={0} | all-to-all | bytes 589824 | tf_op jit(solution)/shard_map/all_to_all | solution.py:158
  32.4 1.3 %shard_map.110 = bf16[16,32,128]{2,1,0:T(8,128)(2,1)} custom-call(bf16[16,72,128]{2,1,0:T(8,128)(2,1)S(1)} %all_to_all.15.in_ref.spectra_ref), custom_call_target="tpu_custom_call" | custom-call | flops 16777216 | bytes 1048576 | tf_op jit(solution)/shard_map/pallas_call | solution.py:247
  33.7 13.7 %all-to-all-start.1 = ((bf16[16,32,128]{2,1,0:T(8,128)(2,1)}), bf16[16,32,128]{2,1,0:T(8,128)(2,1)S(1)}, u32[]{:S(2)}, u32[]{:S(2)}) async-start(bf16[16,32,128]{2,1,0:T(8,128)(2,1)} %shard_map.110), calls=%async_computation.1 | async-start | bytes 262144 | tf_op jit(solution)/shard_map/all_to_all | solution.py:158
  47.4 0.0 copy-done.5
  47.4 0.0 copy-done
  47.5 0.0 copy-done.6
  47.5 1.4 %shard_map.111 = (f32[4,64,128]{2,1,0:T(8,128)S(1)}, f32[4,64,128]{2,1,0:T(8,128)S(1)}) custom-call(bf16[3,4,8192]{2,1,0:T(4,128)(2,1)S(1)} %copy-done, f32[3,4,3]{2,1,0:T(4,128)S(1)} %copy-done.5, bf16[16,72,128]{2,1,0:T(8,128)(2,1)S(1)} %all_to_all.15.in_ref.spectra_ref, f32[4]{0:T(128)S(1)} %copy-done.6), custom_call_target="tpu_custom_call" | custom-call | flops 16777216 | bytes 1048576 | tf_op jit(solution)/shard_map/pallas_call | solution.py:247
  48.9 0.0 copy-start.7
  48.9 3.1 %all-to-all-done.1.in_ref = bf16[16,32,128]{2,1,0:T(8,128)(2,1)S(1)} async-done(((bf16[16,32,128]{2,1,0:T(8,128)(2,1)}), bf16[16,32,128]{2,1,0:T(8,128)(2,1)S(1)}, u32[]{:S(2)}, u32[]{:S(2)}) %all-to-all-start.1) | async-done | bytes 131104 | tf_op jit(solution)/shard_map/all_to_all | solution.py:158
  52.0 0.0 copy-done.1
  52.0 0.0 copy-done.2
  52.0 0.0 copy-done.3
  52.0 0.0 copy-done.4
  52.0 0.5 shard_map.112
  52.5 16.7 %all_to_all.16 = bf16[16,256,128]{2,1,0:T(8,128)(2,1)S(1)} all-to-all(bf16[16,256,128]{2,1,0:T(8,128)(2,1)S(1)} %shard_map.112), channel_id=1, replica_groups={{28,30,0,2,4,6,8,10,12,14,16,18,20,22,24,26},{29,31,1,3,5,7,9,11,13,15,..., dimensions={0} | all-to-all | bytes 2097152 | tf_op jit(solution)/shard_map/all_to_all | solution.py:316
  69.2 6.9 %collective-permute-start = (bf16[16,256,128]{2,1,0:T(8,128)(2,1)S(1)}, bf16[16,256,128]{2,1,0:T(8,128)(2,1)S(1)}, u32[]{:S(2)}, u32[]{:S(2)}) collective-permute-start(bf16[16,256,128]{2,1,0:T(8,128)(2,1)S(1)} %all_to_all.16), channel_id=1, source_target_pairs={{0,1},{1,0},{2,3},{3,2},{4,5},{5,4},{6,7},{7,6},{8,9},{9,8},{10,11... | collective-permute-start | bytes 3145736 | tf_op jit(solution)/shard_map/ppermute | solution.py:317
  76.1 0.0 copy-done.7
  76.2 0.5 concatenate.12
  76.7 0.4 concatenate.11
  77.1 0.5 reshape.71
  77.6 0.8 collective-permute-done
  78.4 0.5 reshape.72
  78.9 2.1 %convolution_convert_fusion = bf16[8192,128]{1,0:T(8,128)(2,1)} fusion(bf16[64,8192]{1,0:T(8,128)(2,1)S(1)} %reshape.72, bf16[64,8192]{1,0:T(8,128)(2,1)S(1)} %reshape.71, bf16[128,128]{1,0:T(8,128)(2,1)S(1)} %concatenate.11, bf16[128,128]{1,0:T(8,128)(2,1)S(1)} %concatenate.12, pred[]{:T(512)S(6)} %eq.5), kind=kOutput, calls=%fused_computation | convolution fusion | flops 273694720 | bytes 4259841 | tf_op jit(solution)/shard_map/dot_general | solution.py:322
  (3 shorter events, 0.0 us)
Async XLA Ops:
  0.0 52.0 %copy-start.1 = (f32[128,128]{1,0:T(8,128)S(1)}, f32[128,128]{1,0:T(8,128)}, u32[]{:S(2)}) copy-start(f32[128,128]{1,0:T(8,128)} %constant.33.clone.sin_hbm.sin_ref) | copy-start | bytes 196612
  0.0 52.0 %copy-start.2 = (f32[128,128]{1,0:T(8,128)S(1)}, f32[128,128]{1,0:T(8,128)}, u32[]{:S(2)}) copy-start(f32[128,128]{1,0:T(8,128)} %constant.32.clone.cos_hbm.cos_ref) | copy-start | bytes 196612
  0.0 52.0 %copy-start.3 = (bf16[384,256]{1,0:T(8,128)(2,1)S(1)}, bf16[384,256]{1,0:T(8,128)(2,1)}, u32[]{:S(2)}) copy-start(bf16[384,256]{1,0:T(8,128)(2,1)} %constant.35.clone.inner_ref) | copy-start | bytes 589828
  0.0 52.0 %copy-start.4 = (bf16[64,384]{1,0:T(8,128)(2,1)S(1)}, bf16[64,384]{1,0:T(8,128)(2,1)}, u32[]{:S(2)}) copy-start(bf16[64,384]{1,0:T(8,128)(2,1)} %constant.31.clone.outer_ref) | copy-start | bytes 147460
  0.0 47.4 %copy-start.5 = (f32[3,4,3]{2,1,0:T(4,128)S(1)}, f32[3,4,3]{2,1,0:T(4,128)}, u32[]{:S(2)}) copy-start(f32[3,4,3]{2,1,0:T(4,128)} %taps_ref.1) | copy-start | bytes 436
  0.0 47.4 %copy-start = (bf16[3,4,8192]{2,1,0:T(4,128)(2,1)S(1)}, bf16[3,4,8192]{2,1,0:T(4,128)(2,1)}, u32[]{:S(2)}) copy-start(bf16[3,4,8192]{2,1,0:T(4,128)(2,1)} %feat_hbm.3) | copy-start | bytes 589828
  0.0 47.4 %copy-start.6 = (f32[4]{0:T(128)S(1)}, f32[4]{0:T(128)}, u32[]{:S(2)}) copy-start(f32[4]{0:T(128)} %gain_ref.1) | copy-start | bytes 52
  33.7 18.2 %all-to-all-start.1 = ((bf16[16,32,128]{2,1,0:T(8,128)(2,1)}), bf16[16,32,128]{2,1,0:T(8,128)(2,1)S(1)}, u32[]{:S(2)}, u32[]{:S(2)}) async-start(bf16[16,32,128]{2,1,0:T(8,128)(2,1)} %shard_map.110), calls=%async_computation.1 | async-start | bytes 262144 | tf_op jit(solution)/shard_map/all_to_all | solution.py:158
  48.9 27.3 %copy-start.7 = (bf16[128,128]{1,0:T(8,128)(2,1)S(1)}, bf16[128,128]{1,0:T(8,128)(2,1)}, u32[]{:S(2)}) copy-start(bf16[128,128]{1,0:T(8,128)(2,1)} %param.15) | copy-start | bytes 98308
  69.2 9.1 %collective-permute-start = (bf16[16,256,128]{2,1,0:T(8,128)(2,1)S(1)}, bf16[16,256,128]{2,1,0:T(8,128)(2,1)S(1)}, u32[]{:S(2)}, u32[]{:S(2)}) collective-permute-start(bf16[16,256,128]{2,1,0:T(8,128)(2,1)S(1)} %all_to_all.16), channel_id=1, source_target_pairs={{0,1},{1,0},{2,3},{3,2},{4,5},{5,4},{6,7},{7,6},{8,9},{9,8},{10,11... | collective-permute-start | bytes 3145736 | tf_op jit(solution)/shard_map/ppermute | solution.py:317

commit v6 on v5

--- a/solution.py
+++ b/solution.py
@@ -12,8 +12,9 @@
 N1, N2 = 64, 128
 BLOCK = N1 * N2
 SLICES = 16
-OUT, BACK = 12, 8
-FIRST_CHIP = 14
+OUT = [(j + 12) % SLICES for j in range(SLICES)]
+BACK = [8, 0, 1, 15, 2, 14, 3, 13, 4, 12, 5, 11, 6, 10, 7, 9]
+CHIPS = [(j + 14) % 16 for j in range(16)]
 f32, bf16 = jnp.float32, jnp.bfloat16
 
 
@@ -138,7 +139,7 @@
     copy = pltpu.make_async_copy(feat_hbm, feat_ref, sem)
     copy.start()
     device = lax.axis_index("seq")
-    ends = spectra_ref[(device + SLICES - 1 - OUT) % SLICES, 64:72, :].astype(f32)
+    ends = spectra_ref[slot(jnp.maximum(device - 1, 0), OUT), 64:72, :].astype(f32)
     ends = jnp.where(device > 0, ends, 0.0)
     edges = [pltpu.roll(ends, 2, 1)[:4], ends[:4], ends[4:]]
     copy.wait()
@@ -149,13 +150,14 @@
         direct_ref[c] = gain_ref[c] * rows[4 + c]
 
 
-def slot(block, first):
-    return (block - first) % SLICES
-
-
-def over_seq(value, first):
-    group = [(j + first) % SLICES for j in range(SLICES)]
-    return lax.all_to_all(value, "seq", 0, 0, tiled=True, axis_index_groups=[group])
+def slot(device, order):
+    if isinstance(device, int):
+        return order.index(device)
+    return sum(jnp.where(device == z, j, 0) for j, z in enumerate(order))
+
+
+def over_seq(value, order):
+    return lax.all_to_all(value, "seq", 0, 0, tiled=True, axis_index_groups=[order])
 
 
 def edge_terms(in_ref):
@@ -179,7 +181,7 @@
 def mix_kernel(in_ref, out_ref):
     top = lax.broadcasted_iota(jnp.int32, (8, N2), 0) < 4
     missing = edge_terms(in_ref)
-    wave = wave_at((lax.axis_index("seq") + SLICES - OUT) % SLICES)
+    wave = wave_at(slot(lax.axis_index("seq"), OUT))
     for pair in range(2):
         sums = []
         for side in range(2):
@@ -219,7 +221,7 @@
 def inverse_kernel(in_ref, queries_ref, direct_ref, outer_ref, cos_ref, sin_ref, inner_ref, out_ref):
     turned = []
     for pair in range(2):
-        both = [in_ref[slot(p + OUT, BACK), 16 * pair : 16 * pair + 16, :].astype(f32) for p in range(SLICES)]
+        both = [in_ref[slot(OUT[p], BACK), 16 * pair : 16 * pair + 16, :].astype(f32) for p in range(SLICES)]
         for side in range(2):
             tile = jnp.concatenate([part[8 * side : 8 * side + 8] for part in both], axis=0)
             tile = inner_stage(tile, inner_ref[...])
@@ -232,6 +234,22 @@
         gated = gated.astype(bf16)
         for copy in range(out_ref.shape[0]):
             out_ref[copy, N1 * c : N1 * (c + 1), :] = gated
+
+
+def project_kernel(own_ref, other_ref, weight_ref, out_hbm, out_ref, sems):
+    lines = N1 // sems.shape[0]
+    copies = []
+    for part in range(sems.shape[0]):
+        tokens = pl.ds(part * lines * N2, lines * N2)
+        other = other_ref[:, :, part * lines : (part + 1) * lines, :]
+        other = other.reshape(own_ref.shape[0], lines, N2).reshape(own_ref.shape[0], lines * N2)
+        rows = jnp.concatenate([own_ref[:, tokens], other], axis=0)
+        done = lax.dot_general(rows, weight_ref[...], (((0,), (0,)), ((), ())), preferred_element_type=f32)
+        out_ref[tokens, :] = done.astype(bf16)
+        copies.append(pltpu.make_async_copy(out_ref.at[tokens, :], out_hbm.at[tokens, :], sems.at[part]))
+        copies[-1].start()
+    for copy in copies:
+        copy.wait()
 
 
 vmem = pl.BlockSpec(memory_space=pltpu.VMEM)
@@ -304,8 +322,7 @@
 
 
 def gather_groups(chips):
-    order = [(chip + FIRST_CHIP) % chips for chip in range(chips)]
-    return [[2 * chip + core for chip in order] for core in range(2)]
+    return [[2 * chip + core for chip in CHIPS] for core in range(2)]
 
 
 def shards(features, short_taps, long_filter, skip_gain, out_weight):
@@ -318,9 +335,15 @@
     blocks = out_weight.reshape(chan, 4, N2)
     sides = [jnp.concatenate([blocks[d] for d in groups[g] + groups[1 - g]], axis=0) for g in range(2)]
     weight = jnp.where(lax.axis_index("chan") % 2 == 0, sides[0], sides[1])
-    rows = jnp.concatenate([own.reshape(4 * chips, BLOCK), other.reshape(4 * chips, BLOCK)], axis=0)
-    projected = lax.dot_general(rows, weight, (((0,), (0,)), ((), ())), preferred_element_type=f32)
-    return projected.astype(bf16)
+    return pl.pallas_call(
+        project_kernel,
+        out_shape=jax.ShapeDtypeStruct((BLOCK, N2), bf16),
+        in_specs=[vmem] * 3,
+        out_specs=hbm,
+        scratch_shapes=[pltpu.VMEM((BLOCK, N2), bf16), pltpu.SemaphoreType.DMA((8,))],
+        compiler_params=pltpu.CompilerParams(vmem_limit_bytes=24 << 20),
+        cost_estimate=pl.CostEstimate(flops=1 << 28, bytes_accessed=1 << 22, transcendentals=0),
+    )(own.reshape(4 * chips, BLOCK), other.reshape(chips, 4, N1, N2), weight)
 
 
 def solution(mesh):

time: 81.2 us -> 79.8 us (0.983)
  matrix products: 2.07 us -> 0 us
  Pallas kernels: 5.35 us -> 7.17 us
    dot_general x1 -> x0, matrix products: 2.07 us -> none  [shards(): lax.dot_general(rows, weight, (((0,), (0,)), ((), ())), preferred_element...]
    pallas_call x0 -> x1, Pallas kernels: none -> 1.82 us  [shards(): pl.pallas_call(project_kernel, out_shape=jax.ShapeDtypeStruct((BLOCK, N2)...]
where the time goes in v6:
time: 79.8 us; the launch traced here: 79.5 us
  blocking collectives  46.9 us (59%)
  starting transfers between devices  20.6 us (26%)
  Pallas kernels  7.17 us (9%)
  waiting for transfers between devices  3.08 us (4%)
  local copies, waits for them, and re-layouts  1.5 us (2%)
    all_to_all x1, blocking collectives, over_seq(): lax.all_to_all(value, 'seq', 0, 0, tiled=True, axis_index_groups=[order])  30.3 us
    all_to_all x1, blocking collectives, shards(): lax.all_to_all(sent, 'chan', 0, 0, tiled=True, axis_index_groups=groups)  16.7 us
    all_to_all x1, starting transfers between devices, over_seq(): lax.all_to_all(value, 'seq', 0, 0, tiled=True, axis_index_groups=[order])  13.7 us
    ppermute x1, starting transfers between devices, shards(): other = lax.ppermute(own, 'chan', [(d, d ^ 1) for d in range(chan)])  6.93 us
    pallas_call x4, Pallas kernels, call(): pl.pallas_call(kernel, out_shape=out_shape, in_specs=specs, out_specs=out...  5.36 us
    all_to_all x1, waiting for transfers between devices, over_seq(): lax.all_to_all(value, 'seq', 0, 0, tiled=True, axis_index_groups=[order])  2.34 us
    pallas_call x1, Pallas kernels, shards(): pl.pallas_call(project_kernel, out_shape=jax.ShapeDtypeStruct((BLOCK, N2)...  1.82 us
  transfers between devices with their start and end apart: 2, of which 2 were waited for; matrix products, arithmetic and copies ran while one was open for 2% of the time, Pallas kernels for 2%

profile of v6, /device:TPU:1, one launch (start us, length us, event | category | flops | bytes accessed | tf_op | source)
XLA Modules:
  0.0 79.5 jit_solution(14461488184357609076)
XLA Ops:
  0.0 0.0 copy-start.1
  0.0 0.0 copy-start.2
  0.0 0.0 copy-start.3
  0.0 0.0 copy-start.4
  0.0 0.0 copy-start.5
  0.0 0.0 copy-start
  0.0 0.0 copy-start.6
  0.1 2.1 %shard_map.109 = bf16[16,72,128]{2,1,0:T(8,128)(2,1)S(1)} custom-call(bf16[3,4,8192]{2,1,0:T(4,128)(2,1)} %feat_hbm.3, f32[3,4,3]{2,1,0:T(4,128)} %taps_ref.1, f32[4,8192]{1,0:T(4,128)} %filt_hbm.1, bf16[128,192]{1,0:T(8,128)(2,1)} %constant.30.clone.outer_hbm, f32[128,128]{1,0:T(8,128)} %constant.32.clone.cos_hbm.cos_ref, ...), custom_call_target="tpu_custom_call" | custom-call | flops 16777216 | bytes 1048576 | tf_op jit(solution)/shard_map/pallas_call | solution.py:265
  2.2 30.3 %all_to_all.15.in_ref.spectra_ref = bf16[16,72,128]{2,1,0:T(8,128)(2,1)S(1)} all-to-all(bf16[16,72,128]{2,1,0:T(8,128)(2,1)S(1)} %shard_map.109), channel_id=1, replica_groups={{384,416,448,480,0,32,64,96,128,160,192,224,256,288,320,352},{385,417,4..., dimensions={0} | all-to-all | bytes 589824 | tf_op jit(solution)/shard_map/all_to_all | solution.py:160
  32.4 1.3 %shard_map.110 = bf16[16,32,128]{2,1,0:T(8,128)(2,1)} custom-call(bf16[16,72,128]{2,1,0:T(8,128)(2,1)S(1)} %all_to_all.15.in_ref.spectra_ref), custom_call_target="tpu_custom_call" | custom-call | flops 16777216 | bytes 1048576 | tf_op jit(solution)/shard_map/pallas_call | solution.py:265
  33.7 13.7 %all-to-all-start.1 = ((bf16[16,32,128]{2,1,0:T(8,128)(2,1)}), bf16[16,32,128]{2,1,0:T(8,128)(2,1)S(1)}, u32[]{:S(2)}, u32[]{:S(2)}) async-start(bf16[16,32,128]{2,1,0:T(8,128)(2,1)} %shard_map.110), calls=%async_computation.1 | async-start | bytes 262144 | tf_op jit(solution)/shard_map/all_to_all | solution.py:160
  47.4 0.0 copy-done.5
  47.4 0.0 copy-done
  47.5 0.0 copy-done.6
  47.5 1.4 %shard_map.111 = (f32[4,64,128]{2,1,0:T(8,128)S(1)}, f32[4,64,128]{2,1,0:T(8,128)S(1)}) custom-call(bf16[3,4,8192]{2,1,0:T(4,128)(2,1)S(1)} %copy-done, f32[3,4,3]{2,1,0:T(4,128)S(1)} %copy-done.5, bf16[16,72,128]{2,1,0:T(8,128)(2,1)S(1)} %all_to_all.15.in_ref.spectra_ref, f32[4]{0:T(128)S(1)} %copy-done.6), custom_call_target="tpu_custom_call" | custom-call | flops 16777216 | bytes 1048576 | tf_op jit(solution)/shard_map/pallas_call | solution.py:265
  48.9 0.0 copy-start.7
  48.9 2.3 %all-to-all-done.1.in_ref = bf16[16,32,128]{2,1,0:T(8,128)(2,1)S(1)} async-done(((bf16[16,32,128]{2,1,0:T(8,128)(2,1)}), bf16[16,32,128]{2,1,0:T(8,128)(2,1)S(1)}, u32[]{:S(2)}, u32[]{:S(2)}) %all-to-all-start.1) | async-done | bytes 131104 | tf_op jit(solution)/shard_map/all_to_all | solution.py:160
  51.2 0.0 copy-done.1
  51.2 0.0 copy-done.2
  51.2 0.0 copy-done.3
  51.3 0.0 copy-done.4
  51.3 0.5 shard_map.112
  51.8 16.7 %all_to_all.16 = bf16[16,256,128]{2,1,0:T(8,128)(2,1)S(1)} all-to-all(bf16[16,256,128]{2,1,0:T(8,128)(2,1)S(1)} %shard_map.112), channel_id=1, replica_groups={{28,30,0,2,4,6,8,10,12,14,16,18,20,22,24,26},{29,31,1,3,5,7,9,11,13,15,..., dimensions={0} | all-to-all | bytes 2097152 | tf_op jit(solution)/shard_map/all_to_all | solution.py:333
  68.4 6.9 %collective-permute-start = (bf16[16,256,128]{2,1,0:T(8,128)(2,1)S(1)}, bf16[16,256,128]{2,1,0:T(8,128)(2,1)S(1)}, u32[]{:S(2)}, u32[]{:S(2)}) collective-permute-start(bf16[16,256,128]{2,1,0:T(8,128)(2,1)S(1)} %all_to_all.16), channel_id=1, source_target_pairs={{0,1},{1,0},{2,3},{3,2},{4,5},{5,4},{6,7},{7,6},{8,9},{9,8},{10,11... | collective-permute-start | bytes 3145736 | tf_op jit(solution)/shard_map/ppermute | solution.py:334
  75.4 0.0 copy-done.7
  75.5 0.5 concatenate.8
  76.0 0.4 concatenate.7
  76.4 0.5 reshape.71.own_ref
  76.9 0.7 collective-permute-done
  77.7 1.8 %shard_map.113 = bf16[8192,128]{1,0:T(8,128)(2,1)} custom-call(bf16[64,8192]{1,0:T(8,128)(2,1)S(1)} %reshape.71.own_ref, bf16[16,4,64,128]{3,2,1,0:T(8,128)(2,1)S(1)} %bitcast.1, bf16[128,128]{1,0:T(8,128)(2,1)S(1)} %broadcast_select_fusion.weight_ref), custom_call_target="tpu_custom_call" | custom-call | flops 268435456 | bytes 4194304 | tf_op jit(solution)/shard_map/pallas_call | solution.py:338
  (4 shorter events, 0.0 us)
Async XLA Ops:
  0.0 51.2 %copy-start.1 = (f32[128,128]{1,0:T(8,128)S(1)}, f32[128,128]{1,0:T(8,128)}, u32[]{:S(2)}) copy-start(f32[128,128]{1,0:T(8,128)} %constant.33.clone.sin_hbm.sin_ref) | copy-start | bytes 196612
  0.0 51.2 %copy-start.2 = (f32[128,128]{1,0:T(8,128)S(1)}, f32[128,128]{1,0:T(8,128)}, u32[]{:S(2)}) copy-start(f32[128,128]{1,0:T(8,128)} %constant.32.clone.cos_hbm.cos_ref) | copy-start | bytes 196612
  0.0 51.2 %copy-start.3 = (bf16[384,256]{1,0:T(8,128)(2,1)S(1)}, bf16[384,256]{1,0:T(8,128)(2,1)}, u32[]{:S(2)}) copy-start(bf16[384,256]{1,0:T(8,128)(2,1)} %constant.35.clone.inner_ref) | copy-start | bytes 589828
  0.0 51.2 %copy-start.4 = (bf16[64,384]{1,0:T(8,128)(2,1)S(1)}, bf16[64,384]{1,0:T(8,128)(2,1)}, u32[]{:S(2)}) copy-start(bf16[64,384]{1,0:T(8,128)(2,1)} %constant.31.clone.outer_ref) | copy-start | bytes 147460
  0.0 47.4 %copy-start.5 = (f32[3,4,3]{2,1,0:T(4,128)S(1)}, f32[3,4,3]{2,1,0:T(4,128)}, u32[]{:S(2)}) copy-start(f32[3,4,3]{2,1,0:T(4,128)} %taps_ref.1) | copy-start | bytes 436
  0.0 47.4 %copy-start = (bf16[3,4,8192]{2,1,0:T(4,128)(2,1)S(1)}, bf16[3,4,8192]{2,1,0:T(4,128)(2,1)}, u32[]{:S(2)}) copy-start(bf16[3,4,8192]{2,1,0:T(4,128)(2,1)} %feat_hbm.3) | copy-start | bytes 589828
  0.0 47.4 %copy-start.6 = (f32[4]{0:T(128)S(1)}, f32[4]{0:T(128)}, u32[]{:S(2)}) copy-start(f32[4]{0:T(128)} %gain_ref.1) | copy-start | bytes 52
  33.7 17.5 %all-to-all-start.1 = ((bf16[16,32,128]{2,1,0:T(8,128)(2,1)}), bf16[16,32,128]{2,1,0:T(8,128)(2,1)S(1)}, u32[]{:S(2)}, u32[]{:S(2)}) async-start(bf16[16,32,128]{2,1,0:T(8,128)(2,1)} %shard_map.110), calls=%async_computation.1 | async-start | bytes 262144 | tf_op jit(solution)/shard_map/all_to_all | solution.py:160
  48.9 26.5 %copy-start.7 = (bf16[128,128]{1,0:T(8,128)(2,1)S(1)}, bf16[128,128]{1,0:T(8,128)(2,1)}, u32[]{:S(2)}) copy-start(bf16[128,128]{1,0:T(8,128)(2,1)} %param.15) | copy-start | bytes 98308
  68.4 9.2 %collective-permute-start = (bf16[16,256,128]{2,1,0:T(8,128)(2,1)S(1)}, bf16[16,256,128]{2,1,0:T(8,128)(2,1)S(1)}, u32[]{:S(2)}, u32[]{:S(2)}) collective-permute-start(bf16[16,256,128]{2,1,0:T(8,128)(2,1)S(1)} %all_to_all.16), channel_id=1, source_target_pairs={{0,1},{1,0},{2,3},{3,2},{4,5},{5,4},{6,7},{7,6},{8,9},{9,8},{10,11... | collective-permute-start | bytes 3145736 | tf_op jit(solution)/shard_map/ppermute | solution.py:334

commit v7 on v6

--- a/solution.py
+++ b/solution.py
@@ -116,9 +116,10 @@
     for copy in copies[:4]:
         copy.wait()
     streams = [feat_ref[i].astype(f32) for i in range(2)]
-    ends = block_ends(last_ref[...].astype(f32), streams, taps_ref).astype(bf16)
+    ends = block_ends(last_ref[...].astype(f32), streams, taps_ref)
+    ends = jnp.concatenate([ends, jnp.zeros_like(ends)], axis=0).astype(bf16)
     for device in range(SLICES):
-        out_ref[device, 64:72, :] = ends
+        out_ref[device, 64:80, :] = ends
     product = short_filter(streams[0], taps_ref[1]) * short_filter(streams[1], taps_ref[2])
     signals = to_blocks(product, filt_ref[...], rows_ref)
     high, low = split(jnp.concatenate(signals, axis=1))
@@ -139,7 +140,7 @@
     copy = pltpu.make_async_copy(feat_hbm, feat_ref, sem)
     copy.start()
     device = lax.axis_index("seq")
-    ends = spectra_ref[slot(jnp.maximum(device - 1, 0), OUT), 64:72, :].astype(f32)
+    ends = spectra_ref[slot(jnp.maximum(device - 1, 0), OUT), 64:80, :].astype(f32)[:8]
     ends = jnp.where(device > 0, ends, 0.0)
     edges = [pltpu.roll(ends, 2, 1)[:4], ends[:4], ends[4:]]
     copy.wait()
@@ -163,7 +164,7 @@
 def edge_terms(in_ref):
     missing, given = [None], None
     for block in range(SLICES):
-        ends = in_ref[slot(block, OUT), 64:72, :].astype(f32)
+        ends = in_ref[slot(block, OUT), 64:80, :].astype(f32)[:8]
         own = ends + pltpu.roll(ends, N1, 1)
         if block:
             missing.append(own * pltpu.roll(given, 4, 0) + given * pltpu.roll(own + given, 4, 0))
@@ -197,13 +198,14 @@
                 both = in_ref[slot(block, OUT), 32 + 16 * pair : 48 + 16 * pair, :].astype(f32)
                 filt.append(both[8 * side : 8 * side + 8])
             swapped = [pltpu.roll(tile, 4, 0) for tile in data]
+            filter_swapped = [pltpu.roll(tile, 4, 0) for tile in filt]
             real_parts, imag_parts = [], []
             for m in range(SLICES):
-                tile = filt[m]
+                tile, turned = filt[m], filter_swapped[m]
                 if m:
-                    turned = pltpu.roll(filt[m - 1], 4, 0)
-                    tile = tile + jnp.where(top, -turned, turned)
-                turned = pltpu.roll(tile, 4, 0)
+                    last = filter_swapped[m - 1]
+                    tile = tile + jnp.where(top, -last, last)
+                    turned = turned + jnp.where(top, filt[m - 1], -filt[m - 1])
                 real_parts.append(jnp.where(top, tile, turned))
                 imag_parts.append(jnp.where(top, -turned, tile))
             row = []
@@ -281,7 +283,7 @@
     spectra = call(
         forward_kernel,
         [hbm] * 7,
-        (SLICES, 72, N2),
+        (SLICES, 80, N2),
         bf16,
         *held,
         scratch=[pltpu.VMEM((2, 4, BLOCK), bf16)]

time: 79.8 us -> 81.2 us (1.018)
  blocking collectives: 46.9 us -> 47.9 us
    all_to_all x1, blocking collectives: 30.3 us -> 31.2 us  [over_seq(): lax.all_to_all(value, 'seq', 0, 0, tiled=True, axis_index_groups=[order])]
where the time goes in v7:
time: 81.2 us; the launch traced here: 80.9 us
  blocking collectives  47.9 us (59%)
  starting transfers between devices  21.1 us (26%)
  Pallas kernels  7.19 us (9%)
  waiting for transfers between devices  3.08 us (4%)
  local copies, waits for them, and re-layouts  1.5 us (2%)
    all_to_all x1, blocking collectives, over_seq(): lax.all_to_all(value, 'seq', 0, 0, tiled=True, axis_index_groups=[order])  31.2 us
    all_to_all x1, blocking collectives, shards(): lax.all_to_all(sent, 'chan', 0, 0, tiled=True, axis_index_groups=groups)  16.7 us
    all_to_all x1, starting transfers between devices, over_seq(): lax.all_to_all(value, 'seq', 0, 0, tiled=True, axis_index_groups=[order])  14.2 us
    ppermute x1, starting transfers between devices, shards(): other = lax.ppermute(own, 'chan', [(d, d ^ 1) for d in range(chan)])  6.9 us
    pallas_call x4, Pallas kernels, call(): pl.pallas_call(kernel, out_shape=out_shape, in_specs=specs, out_specs=out...  5.38 us
    all_to_all x1, waiting for transfers between devices, over_seq(): lax.all_to_all(value, 'seq', 0, 0, tiled=True, axis_index_groups=[order])  2.34 us
    pallas_call x1, Pallas kernels, shards(): pl.pallas_call(project_kernel, out_shape=jax.ShapeDtypeStruct((BLOCK, N2)...  1.82 us
  transfers between devices with their start and end apart: 2, of which 2 were waited for; matrix products, arithmetic and copies ran while one was open for 2% of the time, Pallas kernels for 2%

profile of v7, /device:TPU:1, one launch (start us, length us, event | category | flops | bytes accessed | tf_op | source)
XLA Modules:
  0.0 80.9 jit_solution(1202156126851477496)
XLA Ops:
  0.0 0.0 copy-start.1
  0.0 0.0 copy-start.2
  0.0 0.0 copy-start.3
  0.0 0.0 copy-start.4
  0.0 0.0 copy-start.5
  0.0 0.0 copy-start
  0.0 0.0 copy-start.6
  0.1 2.1 %shard_map.109 = bf16[16,80,128]{2,1,0:T(8,128)(2,1)S(1)} custom-call(bf16[3,4,8192]{2,1,0:T(4,128)(2,1)} %feat_hbm.3, f32[3,4,3]{2,1,0:T(4,128)} %taps_ref.1, f32[4,8192]{1,0:T(4,128)} %filt_hbm.1, bf16[128,192]{1,0:T(8,128)(2,1)} %constant.30.clone.outer_hbm, f32[128,128]{1,0:T(8,128)} %constant.32.clone.cos_hbm.cos_ref, ...), custom_call_target="tpu_custom_call" | custom-call | flops 16777216 | bytes 1048576 | tf_op jit(solution)/shard_map/pallas_call | solution.py:267
  2.2 31.2 %all_to_all.15.in_ref.spectra_ref = bf16[16,80,128]{2,1,0:T(8,128)(2,1)S(1)} all-to-all(bf16[16,80,128]{2,1,0:T(8,128)(2,1)S(1)} %shard_map.109), channel_id=1, replica_groups={{384,416,448,480,0,32,64,96,128,160,192,224,256,288,320,352},{385,417,4..., dimensions={0} | all-to-all | bytes 655360 | tf_op jit(solution)/shard_map/all_to_all | solution.py:161
  33.3 1.3 %shard_map.110 = bf16[16,32,128]{2,1,0:T(8,128)(2,1)} custom-call(bf16[16,80,128]{2,1,0:T(8,128)(2,1)S(1)} %all_to_all.15.in_ref.spectra_ref), custom_call_target="tpu_custom_call" | custom-call | flops 16777216 | bytes 1048576 | tf_op jit(solution)/shard_map/pallas_call | solution.py:267
  34.7 14.2 %all-to-all-start.1 = ((bf16[16,32,128]{2,1,0:T(8,128)(2,1)}), bf16[16,32,128]{2,1,0:T(8,128)(2,1)S(1)}, u32[]{:S(2)}, u32[]{:S(2)}) async-start(bf16[16,32,128]{2,1,0:T(8,128)(2,1)} %shard_map.110), calls=%async_computation.1 | async-start | bytes 262144 | tf_op jit(solution)/shard_map/all_to_all | solution.py:161
  48.9 0.0 copy-done.5
  48.9 0.0 copy-done
  48.9 0.0 copy-done.6
  48.9 1.4 %shard_map.111 = (f32[4,64,128]{2,1,0:T(8,128)S(1)}, f32[4,64,128]{2,1,0:T(8,128)S(1)}) custom-call(bf16[3,4,8192]{2,1,0:T(4,128)(2,1)S(1)} %copy-done, f32[3,4,3]{2,1,0:T(4,128)S(1)} %copy-done.5, bf16[16,80,128]{2,1,0:T(8,128)(2,1)S(1)} %all_to_all.15.in_ref.spectra_ref, f32[4]{0:T(128)S(1)} %copy-done.6), custom_call_target="tpu_custom_call" | custom-call | flops 16777216 | bytes 1048576 | tf_op jit(solution)/shard_map/pallas_call | solution.py:267
  50.4 0.0 copy-start.7
  50.4 2.3 %all-to-all-done.1.in_ref = bf16[16,32,128]{2,1,0:T(8,128)(2,1)S(1)} async-done(((bf16[16,32,128]{2,1,0:T(8,128)(2,1)}), bf16[16,32,128]{2,1,0:T(8,128)(2,1)S(1)}, u32[]{:S(2)}, u32[]{:S(2)}) %all-to-all-start.1) | async-done | bytes 131104 | tf_op jit(solution)/shard_map/all_to_all | solution.py:161
  52.7 0.0 copy-done.1
  52.7 0.0 copy-done.2
  52.7 0.0 copy-done.3
  52.7 0.0 copy-done.4
  52.7 0.5 shard_map.112
  53.2 16.7 %all_to_all.16 = bf16[16,256,128]{2,1,0:T(8,128)(2,1)S(1)} all-to-all(bf16[16,256,128]{2,1,0:T(8,128)(2,1)S(1)} %shard_map.112), channel_id=1, replica_groups={{28,30,0,2,4,6,8,10,12,14,16,18,20,22,24,26},{29,31,1,3,5,7,9,11,13,15,..., dimensions={0} | all-to-all | bytes 2097152 | tf_op jit(solution)/shard_map/all_to_all | solution.py:335
  69.9 6.9 %collective-permute-start = (bf16[16,256,128]{2,1,0:T(8,128)(2,1)S(1)}, bf16[16,256,128]{2,1,0:T(8,128)(2,1)S(1)}, u32[]{:S(2)}, u32[]{:S(2)}) collective-permute-start(bf16[16,256,128]{2,1,0:T(8,128)(2,1)S(1)} %all_to_all.16), channel_id=1, source_target_pairs={{0,1},{1,0},{2,3},{3,2},{4,5},{5,4},{6,7},{7,6},{8,9},{9,8},{10,11... | collective-permute-start | bytes 3145736 | tf_op jit(solution)/shard_map/ppermute | solution.py:336
  76.9 0.0 copy-done.7
  76.9 0.5 concatenate.8
  77.4 0.4 concatenate.7
  77.9 0.5 reshape.71.own_ref
  78.4 0.7 collective-permute-done
  79.1 1.8 %shard_map.113 = bf16[8192,128]{1,0:T(8,128)(2,1)} custom-call(bf16[64,8192]{1,0:T(8,128)(2,1)S(1)} %reshape.71.own_ref, bf16[16,4,64,128]{3,2,1,0:T(8,128)(2,1)S(1)} %bitcast.1, bf16[128,128]{1,0:T(8,128)(2,1)S(1)} %broadcast_select_fusion.weight_ref), custom_call_target="tpu_custom_call" | custom-call | flops 268435456 | bytes 4194304 | tf_op jit(solution)/shard_map/pallas_call | solution.py:340
  (4 shorter events, 0.0 us)
Async XLA Ops:
  0.0 52.7 %copy-start.1 = (f32[128,128]{1,0:T(8,128)S(1)}, f32[128,128]{1,0:T(8,128)}, u32[]{:S(2)}) copy-start(f32[128,128]{1,0:T(8,128)} %constant.33.clone.sin_hbm.sin_ref) | copy-start | bytes 196612
  0.0 52.7 %copy-start.2 = (f32[128,128]{1,0:T(8,128)S(1)}, f32[128,128]{1,0:T(8,128)}, u32[]{:S(2)}) copy-start(f32[128,128]{1,0:T(8,128)} %constant.32.clone.cos_hbm.cos_ref) | copy-start | bytes 196612
  0.0 52.7 %copy-start.3 = (bf16[384,256]{1,0:T(8,128)(2,1)S(1)}, bf16[384,256]{1,0:T(8,128)(2,1)}, u32[]{:S(2)}) copy-start(bf16[384,256]{1,0:T(8,128)(2,1)} %constant.35.clone.inner_ref) | copy-start | bytes 589828
  0.0 52.7 %copy-start.4 = (bf16[64,384]{1,0:T(8,128)(2,1)S(1)}, bf16[64,384]{1,0:T(8,128)(2,1)}, u32[]{:S(2)}) copy-start(bf16[64,384]{1,0:T(8,128)(2,1)} %constant.31.clone.outer_ref) | copy-start | bytes 147460
  0.0 48.9 %copy-start.5 = (f32[3,4,3]{2,1,0:T(4,128)S(1)}, f32[3,4,3]{2,1,0:T(4,128)}, u32[]{:S(2)}) copy-start(f32[3,4,3]{2,1,0:T(4,128)} %taps_ref.1) | copy-start | bytes 436
  0.0 48.9 %copy-start = (bf16[3,4,8192]{2,1,0:T(4,128)(2,1)S(1)}, bf16[3,4,8192]{2,1,0:T(4,128)(2,1)}, u32[]{:S(2)}) copy-start(bf16[3,4,8192]{2,1,0:T(4,128)(2,1)} %feat_hbm.3) | copy-start | bytes 589828
  0.0 48.9 %copy-start.6 = (f32[4]{0:T(128)S(1)}, f32[4]{0:T(128)}, u32[]{:S(2)}) copy-start(f32[4]{0:T(128)} %gain_ref.1) | copy-start | bytes 52
  34.7 18.0 %all-to-all-start.1 = ((bf16[16,32,128]{2,1,0:T(8,128)(2,1)}), bf16[16,32,128]{2,1,0:T(8,128)(2,1)S(1)}, u32[]{:S(2)}, u32[]{:S(2)}) async-start(bf16[16,32,128]{2,1,0:T(8,128)(2,1)} %shard_map.110), calls=%async_computation.1 | async-start | bytes 262144 | tf_op jit(solution)/shard_map/all_to_all | solution.py:161
  50.4 26.5 %copy-start.7 = (bf16[128,128]{1,0:T(8,128)(2,1)S(1)}, bf16[128,128]{1,0:T(8,128)(2,1)}, u32[]{:S(2)}) copy-start(bf16[128,128]{1,0:T(8,128)(2,1)} %param.15) | copy-start | bytes 98308
  69.9 9.2 %collective-permute-start = (bf16[16,256,128]{2,1,0:T(8,128)(2,1)S(1)}, bf16[16,256,128]{2,1,0:T(8,128)(2,1)S(1)}, u32[]{:S(2)}, u32[]{:S(2)}) collective-permute-start(bf16[16,256,128]{2,1,0:T(8,128)(2,1)S(1)} %all_to_all.16), channel_id=1, source_target_pairs={{0,1},{1,0},{2,3},{3,2},{4,5},{5,4},{6,7},{7,6},{8,9},{9,8},{10,11... | collective-permute-start | bytes 3145736 | tf_op jit(solution)/shard_map/ppermute | solution.py:336

commit v8 on v6

--- a/solution.py
+++ b/solution.py
@@ -42,7 +42,7 @@
 
     def inner(sign):
         high, low = split_table(np.concatenate([np.cos(phase), sign * np.sin(phase)], axis=1))
-        return np.concatenate([high, high, low], axis=0)
+        return np.concatenate([high, low], axis=0)
 
     return forward_outer, inverse_outer, turn_cos, turn_sin, inner(-1.0), inner(1.0)
 
@@ -63,6 +63,7 @@
 
 def inner_stage(rows, table):
     high, low = split(rows)
+    table = jnp.concatenate([table[:N2], table], axis=0)
     both = jnp.dot(jnp.concatenate([high, low, high], axis=1), table, preferred_element_type=f32)
     return both[:, :N2] + imag_sign(rows.shape[0]) * halves_swapped(both[:, N2:])
 
@@ -197,13 +198,14 @@
                 both = in_ref[slot(block, OUT), 32 + 16 * pair : 48 + 16 * pair, :].astype(f32)
                 filt.append(both[8 * side : 8 * side + 8])
             swapped = [pltpu.roll(tile, 4, 0) for tile in data]
+            filter_swapped = [pltpu.roll(tile, 4, 0) for tile in filt]
             real_parts, imag_parts = [], []
             for m in range(SLICES):
-                tile = filt[m]
+                tile, turned = filt[m], filter_swapped[m]
                 if m:
-                    turned = pltpu.roll(filt[m - 1], 4, 0)
-                    tile = tile + jnp.where(top, -turned, turned)
-                turned = pltpu.roll(tile, 4, 0)
+                    last = filter_swapped[m - 1]
+                    tile = tile + jnp.where(top, -last, last)
+                    turned = turned + jnp.where(top, filt[m - 1], -filt[m - 1])
                 real_parts.append(jnp.where(top, tile, turned))
                 imag_parts.append(jnp.where(top, -turned, tile))
             row = []

time: 79.8 us -> 79.8 us (level)
  no operation moved by 1% of the time
where the time goes in v8:
time: 79.8 us; the launch traced here: 79.5 us
  blocking collectives  46.9 us (59%)
  starting transfers between devices  20.6 us (26%)
  Pallas kernels  7.2 us (9%)
  waiting for transfers between devices  3.08 us (4%)
  local copies, waits for them, and re-layouts  1.5 us (2%)
    all_to_all x1, blocking collectives, over_seq(): lax.all_to_all(value, 'seq', 0, 0, tiled=True, axis_index_groups=[order])  30.3 us
    all_to_all x1, blocking collectives, shards(): lax.all_to_all(sent, 'chan', 0, 0, tiled=True, axis_index_groups=groups)  16.7 us
    all_to_all x1, starting transfers between devices, over_seq(): lax.all_to_all(value, 'seq', 0, 0, tiled=True, axis_index_groups=[order])  13.7 us
    ppermute x1, starting transfers between devices, shards(): other = lax.ppermute(own, 'chan', [(d, d ^ 1) for d in range(chan)])  6.91 us
    pallas_call x4, Pallas kernels, call(): pl.pallas_call(kernel, out_shape=out_shape, in_specs=specs, out_specs=out...  5.38 us
    all_to_all x1, waiting for transfers between devices, over_seq(): lax.all_to_all(value, 'seq', 0, 0, tiled=True, axis_index_groups=[order])  2.34 us
    pallas_call x1, Pallas kernels, shards(): pl.pallas_call(project_kernel, out_shape=jax.ShapeDtypeStruct((BLOCK, N2)...  1.82 us
  transfers between devices with their start and end apart: 2, of which 2 were waited for; matrix products, arithmetic and copies ran while one was open for 2% of the time, Pallas kernels for 2%

profile of v8, /device:TPU:1, one launch (start us, length us, event | category | flops | bytes accessed | tf_op | source)
XLA Modules:
  0.0 79.5 jit_solution(9906827033891410199)
XLA Ops:
  0.0 0.0 copy-start.1
  0.0 0.0 copy-start.2
  0.0 0.0 copy-start.3
  0.0 0.0 copy-start.4
  0.0 0.0 copy-start.5
  0.0 0.0 copy-start
  0.0 0.0 copy-start.6
  0.1 2.1 %shard_map.109 = bf16[16,72,128]{2,1,0:T(8,128)(2,1)S(1)} custom-call(bf16[3,4,8192]{2,1,0:T(4,128)(2,1)} %feat_hbm.3, f32[3,4,3]{2,1,0:T(4,128)} %taps_ref.1, f32[4,8192]{1,0:T(4,128)} %filt_hbm.1, bf16[128,192]{1,0:T(8,128)(2,1)} %constant.30.clone.outer_hbm, f32[128,128]{1,0:T(8,128)} %constant.32.clone.cos_hbm.cos_ref, ...), custom_call_target="tpu_custom_call" | custom-call | flops 16777216 | bytes 1048576 | tf_op jit(solution)/shard_map/pallas_call | solution.py:267
  2.2 30.3 %all_to_all.15.in_ref.spectra_ref = bf16[16,72,128]{2,1,0:T(8,128)(2,1)S(1)} all-to-all(bf16[16,72,128]{2,1,0:T(8,128)(2,1)S(1)} %shard_map.109), channel_id=1, replica_groups={{384,416,448,480,0,32,64,96,128,160,192,224,256,288,320,352},{385,417,4..., dimensions={0} | all-to-all | bytes 589824 | tf_op jit(solution)/shard_map/all_to_all | solution.py:161
  32.4 1.3 %shard_map.110 = bf16[16,32,128]{2,1,0:T(8,128)(2,1)} custom-call(bf16[16,72,128]{2,1,0:T(8,128)(2,1)S(1)} %all_to_all.15.in_ref.spectra_ref), custom_call_target="tpu_custom_call" | custom-call | flops 16777216 | bytes 1048576 | tf_op jit(solution)/shard_map/pallas_call | solution.py:267
  33.7 13.7 %all-to-all-start.1 = ((bf16[16,32,128]{2,1,0:T(8,128)(2,1)}), bf16[16,32,128]{2,1,0:T(8,128)(2,1)S(1)}, u32[]{:S(2)}, u32[]{:S(2)}) async-start(bf16[16,32,128]{2,1,0:T(8,128)(2,1)} %shard_map.110), calls=%async_computation.1 | async-start | bytes 262144 | tf_op jit(solution)/shard_map/all_to_all | solution.py:161
  47.4 0.0 copy-done.5
  47.4 0.0 copy-done
  47.5 0.0 copy-done.6
  47.5 0.0 copy-start.7
  47.5 1.4 %shard_map.111 = (f32[4,64,128]{2,1,0:T(8,128)S(1)}, f32[4,64,128]{2,1,0:T(8,128)S(1)}) custom-call(bf16[3,4,8192]{2,1,0:T(4,128)(2,1)S(1)} %copy-done, f32[3,4,3]{2,1,0:T(4,128)S(1)} %copy-done.5, bf16[16,72,128]{2,1,0:T(8,128)(2,1)S(1)} %all_to_all.15.in_ref.spectra_ref, f32[4]{0:T(128)S(1)} %copy-done.6), custom_call_target="tpu_custom_call" | custom-call | flops 16777216 | bytes 1048576 | tf_op jit(solution)/shard_map/pallas_call | solution.py:267
  48.9 2.3 %all-to-all-done.1.in_ref = bf16[16,32,128]{2,1,0:T(8,128)(2,1)S(1)} async-done(((bf16[16,32,128]{2,1,0:T(8,128)(2,1)}), bf16[16,32,128]{2,1,0:T(8,128)(2,1)S(1)}, u32[]{:S(2)}, u32[]{:S(2)}) %all-to-all-start.1) | async-done | bytes 131104 | tf_op jit(solution)/shard_map/all_to_all | solution.py:161
  51.2 0.0 copy-done.1
  51.3 0.0 copy-done.2
  51.3 0.0 copy-done.3
  51.3 0.0 copy-done.4
  51.3 0.5 shard_map.112
  51.8 16.7 %all_to_all.16 = bf16[16,256,128]{2,1,0:T(8,128)(2,1)S(1)} all-to-all(bf16[16,256,128]{2,1,0:T(8,128)(2,1)S(1)} %shard_map.112), channel_id=1, replica_groups={{28,30,0,2,4,6,8,10,12,14,16,18,20,22,24,26},{29,31,1,3,5,7,9,11,13,15,..., dimensions={0} | all-to-all | bytes 2097152 | tf_op jit(solution)/shard_map/all_to_all | solution.py:335
  68.5 6.9 %collective-permute-start = (bf16[16,256,128]{2,1,0:T(8,128)(2,1)S(1)}, bf16[16,256,128]{2,1,0:T(8,128)(2,1)S(1)}, u32[]{:S(2)}, u32[]{:S(2)}) collective-permute-start(bf16[16,256,128]{2,1,0:T(8,128)(2,1)S(1)} %all_to_all.16), channel_id=1, source_target_pairs={{0,1},{1,0},{2,3},{3,2},{4,5},{5,4},{6,7},{7,6},{8,9},{9,8},{10,11... | collective-permute-start | bytes 3145736 | tf_op jit(solution)/shard_map/ppermute | solution.py:336
  75.4 0.0 copy-done.7
  75.5 0.5 concatenate.8
  76.0 0.4 concatenate.7
  76.4 0.5 reshape.71.own_ref
  76.9 0.7 collective-permute-done
  77.7 1.8 %shard_map.113 = bf16[8192,128]{1,0:T(8,128)(2,1)} custom-call(bf16[64,8192]{1,0:T(8,128)(2,1)S(1)} %reshape.71.own_ref, bf16[16,4,64,128]{3,2,1,0:T(8,128)(2,1)S(1)} %bitcast.1, bf16[128,128]{1,0:T(8,128)(2,1)S(1)} %broadcast_select_fusion.weight_ref), custom_call_target="tpu_custom_call" | custom-call | flops 268435456 | bytes 4194304 | tf_op jit(solution)/shard_map/pallas_call | solution.py:340
  (4 shorter events, 0.0 us)
Async XLA Ops:
  0.0 51.2 %copy-start.1 = (f32[128,128]{1,0:T(8,128)S(1)}, f32[128,128]{1,0:T(8,128)}, u32[]{:S(2)}) copy-start(f32[128,128]{1,0:T(8,128)} %constant.33.clone.sin_hbm.sin_ref) | copy-start | bytes 196612
  0.0 51.3 %copy-start.2 = (f32[128,128]{1,0:T(8,128)S(1)}, f32[128,128]{1,0:T(8,128)}, u32[]{:S(2)}) copy-start(f32[128,128]{1,0:T(8,128)} %constant.32.clone.cos_hbm.cos_ref) | copy-start | bytes 196612
  0.0 51.3 %copy-start.3 = (bf16[256,256]{1,0:T(8,128)(2,1)S(1)}, bf16[256,256]{1,0:T(8,128)(2,1)}, u32[]{:S(2)}) copy-start(bf16[256,256]{1,0:T(8,128)(2,1)} %constant.35.clone.inner_ref) | copy-start | bytes 393220
  0.0 51.3 %copy-start.4 = (bf16[64,384]{1,0:T(8,128)(2,1)S(1)}, bf16[64,384]{1,0:T(8,128)(2,1)}, u32[]{:S(2)}) copy-start(bf16[64,384]{1,0:T(8,128)(2,1)} %constant.31.clone.outer_ref) | copy-start | bytes 147460
  0.0 47.4 %copy-start.5 = (f32[3,4,3]{2,1,0:T(4,128)S(1)}, f32[3,4,3]{2,1,0:T(4,128)}, u32[]{:S(2)}) copy-start(f32[3,4,3]{2,1,0:T(4,128)} %taps_ref.1) | copy-start | bytes 436
  0.0 47.4 %copy-start = (bf16[3,4,8192]{2,1,0:T(4,128)(2,1)S(1)}, bf16[3,4,8192]{2,1,0:T(4,128)(2,1)}, u32[]{:S(2)}) copy-start(bf16[3,4,8192]{2,1,0:T(4,128)(2,1)} %feat_hbm.3) | copy-start | bytes 589828
  0.0 47.4 %copy-start.6 = (f32[4]{0:T(128)S(1)}, f32[4]{0:T(128)}, u32[]{:S(2)}) copy-start(f32[4]{0:T(128)} %gain_ref.1) | copy-start | bytes 52
  33.7 17.5 %all-to-all-start.1 = ((bf16[16,32,128]{2,1,0:T(8,128)(2,1)}), bf16[16,32,128]{2,1,0:T(8,128)(2,1)S(1)}, u32[]{:S(2)}, u32[]{:S(2)}) async-start(bf16[16,32,128]{2,1,0:T(8,128)(2,1)} %shard_map.110), calls=%async_computation.1 | async-start | bytes 262144 | tf_op jit(solution)/shard_map/all_to_all | solution.py:161
  47.5 27.9 %copy-start.7 = (bf16[128,128]{1,0:T(8,128)(2,1)S(1)}, bf16[128,128]{1,0:T(8,128)(2,1)}, u32[]{:S(2)}) copy-start(bf16[128,128]{1,0:T(8,128)(2,1)} %param.15) | copy-start | bytes 98308
  68.5 9.2 %collective-permute-start = (bf16[16,256,128]{2,1,0:T(8,128)(2,1)S(1)}, bf16[16,256,128]{2,1,0:T(8,128)(2,1)S(1)}, u32[]{:S(2)}, u32[]{:S(2)}) collective-permute-start(bf16[16,256,128]{2,1,0:T(8,128)(2,1)S(1)} %all_to_all.16), channel_id=1, source_target_pairs={{0,1},{1,0},{2,3},{3,2},{4,5},{5,4},{6,7},{7,6},{8,9},{9,8},{10,11... | collective-permute-start | bytes 3145736 | tf_op jit(solution)/shard_map/ppermute | solution.py:336

commit v9 on v8

--- a/solution.py
+++ b/solution.py
@@ -12,7 +12,7 @@
 N1, N2 = 64, 128
 BLOCK = N1 * N2
 SLICES = 16
-OUT = [(j + 12) % SLICES for j in range(SLICES)]
+OUT = [(j + 10) % SLICES for j in range(SLICES)]
 BACK = [8, 0, 1, 15, 2, 14, 3, 13, 4, 12, 5, 11, 6, 10, 7, 9]
 CHIPS = [(j + 14) % 16 for j in range(16)]
 f32, bf16 = jnp.float32, jnp.bfloat16

time: 79.8 us -> 79.6 us (level)
  starting transfers between devices: 20.6 us -> 18.4 us
  blocking collectives: 46.9 us -> 48.7 us
    all_to_all x1, starting transfers between devices: 13.7 us -> 12.2 us  [over_seq(): lax.all_to_all(value, 'seq', 0, 0, tiled=True, axis_index_groups=[order])]
    all_to_all x1, blocking collectives: 30.3 us -> 31.3 us  [over_seq(): lax.all_to_all(value, 'seq', 0, 0, tiled=True, axis_index_groups=[order])]
where the time goes in v9:
time: 79.6 us; the launch traced here: 79.3 us
  blocking collectives  48.7 us (61%)
  starting transfers between devices  18.4 us (23%)
  Pallas kernels  7.19 us (9%)
  waiting for transfers between devices  3.42 us (4%)
  local copies, waits for them, and re-layouts  1.5 us (2%)
    all_to_all x1, blocking collectives, over_seq(): lax.all_to_all(value, 'seq', 0, 0, tiled=True, axis_index_groups=[order])  31.3 us
    all_to_all x1, blocking collectives, shards(): lax.all_to_all(sent, 'chan', 0, 0, tiled=True, axis_index_groups=groups)  17.4 us
    all_to_all x1, starting transfers between devices, over_seq(): lax.all_to_all(value, 'seq', 0, 0, tiled=True, axis_index_groups=[order])  12.2 us
    ppermute x1, starting transfers between devices, shards(): other = lax.ppermute(own, 'chan', [(d, d ^ 1) for d in range(chan)])  6.23 us
    pallas_call x4, Pallas kernels, call(): pl.pallas_call(kernel, out_shape=out_shape, in_specs=specs, out_specs=out...  5.37 us
    all_to_all x1, waiting for transfers between devices, over_seq(): lax.all_to_all(value, 'seq', 0, 0, tiled=True, axis_index_groups=[order])  2.68 us
    pallas_call x1, Pallas kernels, shards(): pl.pallas_call(project_kernel, out_shape=jax.ShapeDtypeStruct((BLOCK, N2)...  1.82 us
  transfers between devices with their start and end apart: 2, of which 2 were waited for; matrix products, arithmetic and copies ran while one was open for 2% of the time, Pallas kernels for 2%

profile of v9, /device:TPU:1, one launch (start us, length us, event | category | flops | bytes accessed | tf_op | source)
XLA Modules:
  0.0 79.3 jit_solution(2159529580607314471)
XLA Ops:
  0.0 0.0 copy-start.1
  0.0 0.0 copy-start.2
  0.0 0.0 copy-start.3
  0.0 0.0 copy-start.4
  0.0 0.0 copy-start.5
  0.0 0.0 copy-start
  0.0 0.0 copy-start.6
  0.1 2.1 %shard_map.109 = bf16[16,72,128]{2,1,0:T(8,128)(2,1)S(1)} custom-call(bf16[3,4,8192]{2,1,0:T(4,128)(2,1)} %feat_hbm.3, f32[3,4,3]{2,1,0:T(4,128)} %taps_ref.1, f32[4,8192]{1,0:T(4,128)} %filt_hbm.1, bf16[128,192]{1,0:T(8,128)(2,1)} %constant.30.clone.outer_hbm, f32[128,128]{1,0:T(8,128)} %constant.32.clone.cos_hbm.cos_ref, ...), custom_call_target="tpu_custom_call" | custom-call | flops 16777216 | bytes 1048576 | tf_op jit(solution)/shard_map/pallas_call | solution.py:267
  2.2 31.3 %all_to_all.15.in_ref.spectra_ref = bf16[16,72,128]{2,1,0:T(8,128)(2,1)S(1)} all-to-all(bf16[16,72,128]{2,1,0:T(8,128)(2,1)S(1)} %shard_map.109), channel_id=1, replica_groups={{320,352,384,416,448,480,0,32,64,96,128,160,192,224,256,288},{321,353,3..., dimensions={0} | all-to-all | bytes 589824 | tf_op jit(solution)/shard_map/all_to_all | solution.py:161
  33.5 1.3 %shard_map.110 = bf16[16,32,128]{2,1,0:T(8,128)(2,1)} custom-call(bf16[16,72,128]{2,1,0:T(8,128)(2,1)S(1)} %all_to_all.15.in_ref.spectra_ref), custom_call_target="tpu_custom_call" | custom-call | flops 16777216 | bytes 1048576 | tf_op jit(solution)/shard_map/pallas_call | solution.py:267
  34.8 12.2 %all-to-all-start.1 = ((bf16[16,32,128]{2,1,0:T(8,128)(2,1)}), bf16[16,32,128]{2,1,0:T(8,128)(2,1)S(1)}, u32[]{:S(2)}, u32[]{:S(2)}) async-start(bf16[16,32,128]{2,1,0:T(8,128)(2,1)} %shard_map.110), calls=%async_computation.1 | async-start | bytes 262144 | tf_op jit(solution)/shard_map/all_to_all | solution.py:161
  47.0 0.0 copy-done.5
  47.0 0.0 copy-done
  47.0 0.0 copy-done.6
  47.0 0.0 copy-start.7
  47.0 1.4 %shard_map.111 = (f32[4,64,128]{2,1,0:T(8,128)S(1)}, f32[4,64,128]{2,1,0:T(8,128)S(1)}) custom-call(bf16[3,4,8192]{2,1,0:T(4,128)(2,1)S(1)} %copy-done, f32[3,4,3]{2,1,0:T(4,128)S(1)} %copy-done.5, bf16[16,72,128]{2,1,0:T(8,128)(2,1)S(1)} %all_to_all.15.in_ref.spectra_ref, f32[4]{0:T(128)S(1)} %copy-done.6), custom_call_target="tpu_custom_call" | custom-call | flops 16777216 | bytes 1048576 | tf_op jit(solution)/shard_map/pallas_call | solution.py:267
  48.4 2.7 %all-to-all-done.1.in_ref = bf16[16,32,128]{2,1,0:T(8,128)(2,1)S(1)} async-done(((bf16[16,32,128]{2,1,0:T(8,128)(2,1)}), bf16[16,32,128]{2,1,0:T(8,128)(2,1)S(1)}, u32[]{:S(2)}, u32[]{:S(2)}) %all-to-all-start.1) | async-done | bytes 131104 | tf_op jit(solution)/shard_map/all_to_all | solution.py:161
  51.1 0.0 copy-done.1
  51.1 0.0 copy-done.2
  51.1 0.0 copy-done.3
  51.1 0.0 copy-done.4
  51.1 0.5 shard_map.112
  51.7 17.4 %all_to_all.16 = bf16[16,256,128]{2,1,0:T(8,128)(2,1)S(1)} all-to-all(bf16[16,256,128]{2,1,0:T(8,128)(2,1)S(1)} %shard_map.112), channel_id=1, replica_groups={{28,30,0,2,4,6,8,10,12,14,16,18,20,22,24,26},{29,31,1,3,5,7,9,11,13,15,..., dimensions={0} | all-to-all | bytes 2097152 | tf_op jit(solution)/shard_map/all_to_all | solution.py:335
  69.0 6.2 %collective-permute-start = (bf16[16,256,128]{2,1,0:T(8,128)(2,1)S(1)}, bf16[16,256,128]{2,1,0:T(8,128)(2,1)S(1)}, u32[]{:S(2)}, u32[]{:S(2)}) collective-permute-start(bf16[16,256,128]{2,1,0:T(8,128)(2,1)S(1)} %all_to_all.16), channel_id=1, source_target_pairs={{0,1},{1,0},{2,3},{3,2},{4,5},{5,4},{6,7},{7,6},{8,9},{9,8},{10,11... | collective-permute-start | bytes 3145736 | tf_op jit(solution)/shard_map/ppermute | solution.py:336
  75.3 0.0 copy-done.7
  75.3 0.5 concatenate.8
  75.8 0.4 concatenate.7
  76.3 0.5 reshape.71.own_ref
  76.8 0.7 collective-permute-done
  77.5 1.8 %shard_map.113 = bf16[8192,128]{1,0:T(8,128)(2,1)} custom-call(bf16[64,8192]{1,0:T(8,128)(2,1)S(1)} %reshape.71.own_ref, bf16[16,4,64,128]{3,2,1,0:T(8,128)(2,1)S(1)} %bitcast.1, bf16[128,128]{1,0:T(8,128)(2,1)S(1)} %broadcast_select_fusion.weight_ref), custom_call_target="tpu_custom_call" | custom-call | flops 268435456 | bytes 4194304 | tf_op jit(solution)/shard_map/pallas_call | solution.py:340
  (4 shorter events, 0.0 us)
Async XLA Ops:
  0.0 51.1 %copy-start.1 = (f32[128,128]{1,0:T(8,128)S(1)}, f32[128,128]{1,0:T(8,128)}, u32[]{:S(2)}) copy-start(f32[128,128]{1,0:T(8,128)} %constant.33.clone.sin_hbm.sin_ref) | copy-start | bytes 196612
  0.0 51.1 %copy-start.2 = (f32[128,128]{1,0:T(8,128)S(1)}, f32[128,128]{1,0:T(8,128)}, u32[]{:S(2)}) copy-start(f32[128,128]{1,0:T(8,128)} %constant.32.clone.cos_hbm.cos_ref) | copy-start | bytes 196612
  0.0 51.1 %copy-start.3 = (bf16[256,256]{1,0:T(8,128)(2,1)S(1)}, bf16[256,256]{1,0:T(8,128)(2,1)}, u32[]{:S(2)}) copy-start(bf16[256,256]{1,0:T(8,128)(2,1)} %constant.35.clone.inner_ref) | copy-start | bytes 393220
  0.0 51.1 %copy-start.4 = (bf16[64,384]{1,0:T(8,128)(2,1)S(1)}, bf16[64,384]{1,0:T(8,128)(2,1)}, u32[]{:S(2)}) copy-start(bf16[64,384]{1,0:T(8,128)(2,1)} %constant.31.clone.outer_ref) | copy-start | bytes 147460
  0.0 46.9 %copy-start.5 = (f32[3,4,3]{2,1,0:T(4,128)S(1)}, f32[3,4,3]{2,1,0:T(4,128)}, u32[]{:S(2)}) copy-start(f32[3,4,3]{2,1,0:T(4,128)} %taps_ref.1) | copy-start | bytes 436
  0.0 46.9 %copy-start = (bf16[3,4,8192]{2,1,0:T(4,128)(2,1)S(1)}, bf16[3,4,8192]{2,1,0:T(4,128)(2,1)}, u32[]{:S(2)}) copy-start(bf16[3,4,8192]{2,1,0:T(4,128)(2,1)} %feat_hbm.3) | copy-start | bytes 589828
  0.0 46.9 %copy-start.6 = (f32[4]{0:T(128)S(1)}, f32[4]{0:T(128)}, u32[]{:S(2)}) copy-start(f32[4]{0:T(128)} %gain_ref.1) | copy-start | bytes 52
  34.8 16.3 %all-to-all-start.1 = ((bf16[16,32,128]{2,1,0:T(8,128)(2,1)}), bf16[16,32,128]{2,1,0:T(8,128)(2,1)S(1)}, u32[]{:S(2)}, u32[]{:S(2)}) async-start(bf16[16,32,128]{2,1,0:T(8,128)(2,1)} %shard_map.110), calls=%async_computation.1 | async-start | bytes 262144 | tf_op jit(solution)/shard_map/all_to_all | solution.py:161
  47.0 28.3 %copy-start.7 = (bf16[128,128]{1,0:T(8,128)(2,1)S(1)}, bf16[128,128]{1,0:T(8,128)(2,1)}, u32[]{:S(2)}) copy-start(bf16[128,128]{1,0:T(8,128)(2,1)} %param.15) | copy-start | bytes 98308
  69.0 8.5 %collective-permute-start = (bf16[16,256,128]{2,1,0:T(8,128)(2,1)S(1)}, bf16[16,256,128]{2,1,0:T(8,128)(2,1)S(1)}, u32[]{:S(2)}, u32[]{:S(2)}) collective-permute-start(bf16[16,256,128]{2,1,0:T(8,128)(2,1)S(1)} %all_to_all.16), channel_id=1, source_target_pairs={{0,1},{1,0},{2,3},{3,2},{4,5},{5,4},{6,7},{7,6},{8,9},{9,8},{10,11... | collective-permute-start | bytes 3145736 | tf_op jit(solution)/shard_map/ppermute | solution.py:336
